TPU v7x, 32 devices: a whole 2x2x4 slice. The times are simulated.
32 devices in a mesh: dp: 2 (over y), expert: 16 (over z, x, core).
Axes of the slice: x: 2, y: 2, z: 4, core: 2. Of those that a mesh axis runs over, the one named last changes fastest.
Arguments:
- hidden: bfloat16 [16384, 1024], P(('dp', 'expert')), may hold values from -6 to 6
- segments: int32 [16384], P(('dp', 'expert')), may hold values from 0 to 16, never falling along the last dimension, each value on 1 to 2000 neighbouring positions
- routes: int32 [16384, 8], P(('dp', 'expert')), may hold values from 0 to 15, all different within a row
- capacity_blocks: int32 [16], replicated, may hold values from 1 to 2, as said below
- attn_gain: bfloat16 [1024], P('dp'), may hold values from 0.5 to 1.5
- w_query: bfloat16 [1024, 1024], P('dp'), may hold values from -0.375 to 0.375
- key_value_weight: bfloat16 [1024, 1024], P('dp'), may hold values from -0.1875 to 0.1875
- w_out: bfloat16 [1024, 1024], P('dp'), may hold values from -1.5 to 1.5
- ffn_gain: bfloat16 [1024], P('dp'), may hold values from 0.5 to 1.5
- w_router: bfloat16 [1024, 16], P('dp'), may hold values from -0.09375 to 0.09375
- expert_in: bfloat16 [16, 1024, 1024], P('expert', 'dp'), may hold values from -0.1875 to 0.1875
- expert_down: bfloat16 [16, 1024, 512], P('expert', 'dp'), may hold values from -0.75 to 0.75
- cotangent: bfloat16 [16384, 1024], P(('dp', 'expert')), may hold values from -6 to 6
Outputs:
- block_out: bfloat16 [16384, 1024], P(('dp', 'expert'))
- hidden_grad: bfloat16 [16384, 1024], P(('dp', 'expert'))
- attn_gain_grad: float32 [1024], P('dp')
- query_grad: float32 [1024, 1024], P('dp')
- keyval_grad: float32 [1024, 1024], P('dp')
- out_grad: float32 [1024, 1024], P('dp')
- ffn_gain_grad: float32 [1024], P('dp')
- router_grad: float32 [1024, 16], P('dp')
- expert_in_grad: float32 [16, 1024, 1024], P('expert', 'dp')
- expert_down_grad: float32 [16, 1024, 512], P('expert', 'dp')
Inputs may be any that keep to these rules, and one draw needn't show every extreme that they name: `capacity_blocks`: some expert has 1 block and some has 2; a pair beyond its expert's capacity within its sequence is dropped.
All inputs are finite; a program needn't handle non-finite values.
Results may differ from a plain program's by a relative error of at most 0.02.
The roundings to bfloat16 on the way count: a program that leaves them out, or rounds other values in their place, can miss the bound.
Values may be sent and summed in bfloat16 or wider, within the bound.
A program may use at most 320 MiB of HBM per device.

v0:
```python
import jax
import jax.numpy as jnp
from jax import lax
from jax.sharding import PartitionSpec as P

QUERY_HEADS = 16
KEY_VALUE_HEADS = 8
HEAD_DIMENSION = 64
FF = 512
BLOCK_ROWS = 128
CB = 2


norm_eps = 1e-06
theta_base = 10000.0


def rotary_tables(sequence_length, head_dim):
    half_dim = head_dim // 2
    inverse = theta_base ** (-jnp.arange(half_dim, dtype=jnp.float32) * 2.0 / head_dim)
    angles = jnp.arange(sequence_length, dtype=jnp.float32)[:, None] * inverse[None, :]
    angles = jnp.concatenate([angles, angles], axis=-1)
    return (jnp.cos(angles), jnp.sin(angles))


def apply_rotation(value, cosine_lookup, sine_lookup):
    half_dim = value.shape[-1] // 2
    turned = jnp.concatenate([-value[..., half_dim:], value[..., :half_dim]], axis=-1)
    return value * cosine_lookup[:, None, :] + turned * sine_lookup[:, None, :]


def unrotate(grad_val, cosine_lookup, sine_lookup):
    half_dim = grad_val.shape[-1] // 2
    scaled = grad_val * sine_lookup[:, None, :]
    turned = jnp.concatenate([scaled[..., half_dim:], -scaled[..., :half_dim]], axis=-1)
    return grad_val * cosine_lookup[:, None, :] + turned


def masked_scores(query_block, key_rot, block_start, seg_ids, scale):
    span_len = query_block.shape[0]
    raw_scores = (
        jnp.einsum("qkgd,skd->kgqs", query_block, key_rot, preferred_element_type=jnp.float32)
        * scale
    )
    query_pos = block_start + jnp.arange(span_len, dtype=jnp.int32)
    key_pos = jnp.arange(key_rot.shape[0], dtype=jnp.int32)
    allowed = (query_pos[:, None] >= key_pos[None, :]) & (seg_ids[:, None] == seg_ids[None, :])
    return jnp.where(allowed[None, None], raw_scores, -1e30)


def norm_backward(grad_in, gain_vec, normalized, inverse_rms):
    scaled = grad_in * gain_vec
    return inverse_rms * (
        scaled - normalized * jnp.mean(scaled * normalized, axis=-1, keepdims=True)
    )


def on_device(
    hidden,
    segments,
    routes,
    capacity_blocks,
    attn_gain,
    w_query,
    key_value_weight,
    w_out,
    ffn_gain,
    w_router,
    expert_in,
    expert_down,
    cotangent,
):
    sequence_length = hidden.shape[0]
    model_width = hidden.shape[1]
    top_count = routes.shape[1]
    expert_count = capacity_blocks.shape[0]
    owners = lax.axis_size("expert")
    local_count = expert_in.shape[0]
    capacity = BLOCK_ROWS * CB
    group_length = QUERY_HEADS // KEY_VALUE_HEADS
    key_columns = KEY_VALUE_HEADS * HEAD_DIMENSION
    scale = HEAD_DIMENSION ** (-0.5)
    brain_float_half = jnp.bfloat16
    single_float = jnp.float32
    gain_attn, full_query, full_keyval, full_out, gain_ffn, full_router = (
        lax.all_gather(attn_gain, "dp", axis=0, tiled=True),
        lax.all_gather(w_query, "dp", axis=0, tiled=True),
        lax.all_gather(key_value_weight, "dp", axis=0, tiled=True),
        lax.all_gather(w_out, "dp", axis=0, tiled=True),
        lax.all_gather(ffn_gain, "dp", axis=0, tiled=True),
        lax.all_gather(w_router, "dp", axis=0, tiled=True),
    )
    full_in, full_down = (
        lax.all_gather(expert_in, "dp", axis=1, tiled=True),
        lax.all_gather(expert_down, "dp", axis=1, tiled=True),
    )
    gain_attn = gain_attn.astype(single_float)
    gain_ffn = gain_ffn.astype(single_float)
    resid_in = hidden.astype(single_float)
    inverse_one = lax.rsqrt(jnp.mean(resid_in * resid_in, axis=-1, keepdims=True) + norm_eps)
    normal_one = resid_in * inverse_one
    normed = (normal_one * gain_attn).astype(brain_float_half)
    query_pre = jnp.dot(normed, full_query, preferred_element_type=single_float)
    key_value_projected = jnp.dot(normed, full_keyval, preferred_element_type=single_float)
    cosine_lookup, sine_lookup = rotary_tables(sequence_length, HEAD_DIMENSION)
    query_rotated = apply_rotation(
        query_pre.reshape(sequence_length, QUERY_HEADS, HEAD_DIMENSION), cosine_lookup, sine_lookup
    ).astype(brain_float_half)
    key_rot = apply_rotation(
        key_value_projected[:, :key_columns].reshape(
            sequence_length, KEY_VALUE_HEADS, HEAD_DIMENSION
        ),
        cosine_lookup,
        sine_lookup,
    ).astype(brain_float_half)
    value_row_list = (
        key_value_projected[:, key_columns:]
        .reshape(sequence_length, KEY_VALUE_HEADS, HEAD_DIMENSION)
        .astype(brain_float_half)
    )
    block_length = min(512, sequence_length)
    block_total = sequence_length // block_length
    query_block_list = query_rotated.reshape(
        block_total, block_length, KEY_VALUE_HEADS, group_length, HEAD_DIMENSION
    )
    block_starts = jnp.arange(block_total, dtype=jnp.int32) * block_length

    def forward_block(pieces):
        query_block, block_start = pieces
        masked = masked_scores(query_block, key_rot, block_start, segments, scale)
        top_score = jnp.max(masked, axis=-1, keepdims=True)
        log_total = top_score + jnp.log(
            jnp.sum(jnp.exp(masked - top_score), axis=-1, keepdims=True)
        )
        prob_low = jnp.exp(masked - log_total).astype(brain_float_half)
        mixed = jnp.einsum(
            "kgqs,skd->qkgd", prob_low, value_row_list, preferred_element_type=single_float
        )
        return (mixed.astype(brain_float_half), log_total)

    attended_blocks, log_totals = lax.map(forward_block, (query_block_list, block_starts))
    attended = attended_blocks.reshape(sequence_length, QUERY_HEADS * HEAD_DIMENSION)
    first_sum = resid_in + jnp.dot(attended, full_out, preferred_element_type=single_float)
    inverse_two = lax.rsqrt(jnp.mean(first_sum * first_sum, axis=-1, keepdims=True) + norm_eps)
    normal_two = first_sum * inverse_two
    moe_in = (normal_two * gain_ffn).astype(brain_float_half)
    logits = jnp.dot(moe_in, full_router, preferred_element_type=single_float)
    choice_hot = routes[:, :, None] == jnp.arange(expert_count, dtype=jnp.int32)[None, None, :]
    selected = jnp.sum(jnp.where(choice_hot, logits[:, None, :], 0.0), axis=-1)
    gates = jax.nn.softmax(selected, axis=-1)
    flat_routes = routes.reshape(-1)
    hot_table = (flat_routes[:, None] == jnp.arange(expert_count, dtype=jnp.int32)[None, :]).astype(
        jnp.int32
    )
    ranks = jnp.sum(jnp.cumsum(hot_table, axis=0) * hot_table, axis=1) - 1
    limits = BLOCK_ROWS * jnp.sum(hot_table * capacity_blocks[None, :], axis=1)
    kept_flag = ranks < limits
    slot_index = jnp.where(kept_flag, flat_routes * capacity + ranks, expert_count * capacity)
    token_of = jnp.arange(sequence_length * top_count, dtype=jnp.int32) // top_count
    source_row = (
        jnp.full((expert_count * capacity + 1,), sequence_length, jnp.int32)
        .at[slot_index]
        .set(token_of)[:-1]
    )
    kept_mask = kept_flag.reshape(sequence_length, top_count).astype(single_float)
    gate_weight = gates * kept_mask
    moe_pad = jnp.concatenate([moe_in, jnp.zeros((1, model_width), brain_float_half)], axis=0)
    outgoing = moe_pad[source_row].reshape(owners, local_count * capacity, model_width)
    incoming = lax.all_to_all(outgoing, "expert", split_axis=0, concat_axis=0, tiled=True)
    incoming_rows = incoming.reshape(owners, local_count, capacity, model_width)
    gate_up = jnp.einsum(
        "nlcd,ldf->nlcf", incoming_rows, full_in, preferred_element_type=single_float
    )
    gate_part = gate_up[..., :FF]
    up_part = gate_up[..., FF:]
    sigmoid_g = jax.nn.sigmoid(gate_part)
    silu_g = gate_part * sigmoid_g
    expert_hidden = (silu_g * up_part).astype(brain_float_half)
    expert_out = jnp.einsum(
        "nlcf,ldf->nlcd", expert_hidden, full_down, preferred_element_type=single_float
    ).astype(brain_float_half)
    returned = lax.all_to_all(
        expert_out.reshape(owners, local_count * capacity, model_width),
        "expert",
        split_axis=0,
        concat_axis=0,
        tiled=True,
    )
    returned_pad = jnp.concatenate(
        [
            returned.reshape(expert_count * capacity, model_width),
            jnp.zeros((1, model_width), brain_float_half),
        ],
        axis=0,
    )
    routed_rows = returned_pad[slot_index].reshape(sequence_length, top_count, model_width)
    mixture = jnp.sum(routed_rows.astype(single_float) * gate_weight[:, :, None], axis=1)
    block_out = (first_sum + mixture).astype(brain_float_half)
    cot_value = cotangent.astype(single_float)
    gate_grad = kept_mask * jnp.sum(
        routed_rows.astype(single_float) * cot_value[:, None, :], axis=-1
    )
    select_grad = gates * (gate_grad - jnp.sum(gates * gate_grad, axis=-1, keepdims=True))
    logit_grad = jnp.sum(jnp.where(choice_hot, select_grad[:, :, None], 0.0), axis=1).astype(
        brain_float_half
    )
    router_part = jnp.einsum("sd,se->de", moe_in, logit_grad, preferred_element_type=single_float)
    moe_grad = jnp.einsum("se,de->sd", logit_grad, full_router, preferred_element_type=single_float)
    slot_weight = (
        jnp.zeros((expert_count * capacity + 1,), single_float)
        .at[slot_index]
        .set(gate_weight.reshape(-1))[:-1]
    )
    cot_pad = jnp.concatenate([cot_value, jnp.zeros((1, model_width), single_float)], axis=0)
    out_grads = (
        (cot_pad[source_row] * slot_weight[:, None])
        .astype(brain_float_half)
        .reshape(owners, local_count * capacity, model_width)
    )
    grads_here, rows_again = (
        lax.all_to_all(out_grads, "expert", split_axis=0, concat_axis=0, tiled=True),
        lax.all_to_all(outgoing, "expert", split_axis=0, concat_axis=0, tiled=True),
    )
    inputs_here = rows_again.reshape(owners, local_count, capacity, model_width)
    grad_rows = grads_here.reshape(owners, local_count, capacity, model_width)
    hidden_delta = jnp.einsum(
        "nlcd,ldf->nlcf", grad_rows, full_down, preferred_element_type=single_float
    )
    down_part = jnp.einsum(
        "nlcd,nlcf->ldf", grad_rows, expert_hidden, preferred_element_type=single_float
    )
    gate_delta = hidden_delta * up_part * sigmoid_g * (1.0 + gate_part * (1.0 - sigmoid_g))
    up_delta = hidden_delta * silu_g
    gate_up_grad = jnp.concatenate([gate_delta, up_delta], axis=-1).astype(brain_float_half)
    in_part = jnp.einsum(
        "nlcd,nlcf->ldf", inputs_here, gate_up_grad, preferred_element_type=single_float
    )
    row_grads = jnp.einsum(
        "nlcf,ldf->nlcd", gate_up_grad, full_in, preferred_element_type=single_float
    ).astype(brain_float_half)
    grads_back = lax.all_to_all(
        row_grads.reshape(owners, local_count * capacity, model_width),
        "expert",
        split_axis=0,
        concat_axis=0,
        tiled=True,
    )
    grads_pad = jnp.concatenate(
        [
            grads_back.reshape(expert_count * capacity, model_width),
            jnp.zeros((1, model_width), brain_float_half),
        ],
        axis=0,
    )
    moe_grad = moe_grad + jnp.sum(
        grads_pad[slot_index].reshape(sequence_length, top_count, model_width).astype(single_float),
        axis=1,
    )
    ffn_gain_part = jnp.sum(moe_grad * normal_two, axis=0)
    first_grad = cot_value + norm_backward(moe_grad, gain_ffn, normal_two, inverse_two)
    branch_grad = first_grad.astype(brain_float_half)
    out_part = jnp.einsum("sa,sd->ad", attended, branch_grad, preferred_element_type=single_float)
    attended_gradient = jnp.einsum(
        "sd,ad->sa", branch_grad, full_out, preferred_element_type=single_float
    ).astype(brain_float_half)
    gradient_blocks = attended_gradient.reshape(
        block_total, block_length, KEY_VALUE_HEADS, group_length, HEAD_DIMENSION
    )

    def backward_block(carry, pieces):
        key_acc, value_acc = carry
        query_block, grad_block, log_total, block_start = pieces
        masked = masked_scores(query_block, key_rot, block_start, segments, scale)
        probability = jnp.exp(masked - log_total)
        prob_low = probability.astype(brain_float_half)
        prob_grad = jnp.einsum(
            "qkgd,skd->kgqs", grad_block, value_row_list, preferred_element_type=single_float
        )
        row_dot = jnp.sum(probability * prob_grad, axis=-1, keepdims=True)
        score_grad = (probability * (prob_grad - row_dot)).astype(brain_float_half)
        query_delta = (
            jnp.einsum("kgqs,skd->qkgd", score_grad, key_rot, preferred_element_type=single_float)
            * scale
        )
        key_acc = (
            key_acc
            + jnp.einsum(
                "kgqs,qkgd->skd", score_grad, query_block, preferred_element_type=single_float
            )
            * scale
        )
        value_acc = value_acc + jnp.einsum(
            "kgqs,qkgd->skd", prob_low, grad_block, preferred_element_type=single_float
        )
        return ((key_acc, value_acc), query_delta)

    zeroed_rows = jnp.zeros((sequence_length, KEY_VALUE_HEADS, HEAD_DIMENSION), single_float)
    (key_delta, value_delta), query_deltas = lax.scan(
        backward_block,
        (zeroed_rows, zeroed_rows),
        (query_block_list, gradient_blocks, log_totals, block_starts),
    )
    query_grad_low = (
        unrotate(
            query_deltas.reshape(sequence_length, QUERY_HEADS, HEAD_DIMENSION),
            cosine_lookup,
            sine_lookup,
        )
        .astype(brain_float_half)
        .reshape(sequence_length, QUERY_HEADS * HEAD_DIMENSION)
    )
    key_grad_low = unrotate(key_delta, cosine_lookup, sine_lookup).reshape(
        sequence_length, key_columns
    )
    keyval_grad_low = jnp.concatenate(
        [key_grad_low, value_delta.reshape(sequence_length, key_columns)], axis=-1
    ).astype(brain_float_half)
    query_part = jnp.einsum(
        "sd,sa->da", normed, query_grad_low, preferred_element_type=single_float
    )
    keyval_part = jnp.einsum(
        "sd,sa->da", normed, keyval_grad_low, preferred_element_type=single_float
    )
    normed_grad = jnp.einsum(
        "sa,da->sd", query_grad_low, full_query, preferred_element_type=single_float
    )
    normed_grad = normed_grad + jnp.einsum(
        "sa,da->sd", keyval_grad_low, full_keyval, preferred_element_type=single_float
    )
    attn_gain_part = jnp.sum(normed_grad * normal_one, axis=0)
    hidden_grad = (
        first_grad + norm_backward(normed_grad, gain_attn, normal_one, inverse_one)
    ).astype(brain_float_half)
    dense_parts = (attn_gain_part, query_part, keyval_part, out_part, ffn_gain_part, router_part)
    summed = (
        lax.psum(dense_parts[0].astype(jnp.bfloat16), "expert").astype(jnp.float32),
        lax.psum(dense_parts[1].astype(jnp.bfloat16), "expert").astype(jnp.float32),
        lax.psum(dense_parts[2].astype(jnp.bfloat16), "expert").astype(jnp.float32),
        lax.psum(dense_parts[3].astype(jnp.bfloat16), "expert").astype(jnp.float32),
        lax.psum(dense_parts[4].astype(jnp.bfloat16), "expert").astype(jnp.float32),
        lax.psum(dense_parts[5].astype(jnp.bfloat16), "expert").astype(jnp.float32),
    )
    shares = (
        lax.psum_scatter(
            summed[0].astype(jnp.bfloat16), "dp", scatter_dimension=0, tiled=True
        ).astype(jnp.float32),
        lax.psum_scatter(
            summed[1].astype(jnp.bfloat16), "dp", scatter_dimension=0, tiled=True
        ).astype(jnp.float32),
        lax.psum_scatter(
            summed[2].astype(jnp.bfloat16), "dp", scatter_dimension=0, tiled=True
        ).astype(jnp.float32),
        lax.psum_scatter(
            summed[3].astype(jnp.bfloat16), "dp", scatter_dimension=0, tiled=True
        ).astype(jnp.float32),
        lax.psum_scatter(
            summed[4].astype(jnp.bfloat16), "dp", scatter_dimension=0, tiled=True
        ).astype(jnp.float32),
        lax.psum_scatter(
            summed[5].astype(jnp.bfloat16), "dp", scatter_dimension=0, tiled=True
        ).astype(jnp.float32),
    )
    expert_in_share, expert_down_share = (
        lax.psum_scatter(
            in_part.astype(jnp.bfloat16), "dp", scatter_dimension=1, tiled=True
        ).astype(jnp.float32),
        lax.psum_scatter(
            down_part.astype(jnp.bfloat16), "dp", scatter_dimension=1, tiled=True
        ).astype(jnp.float32),
    )
    return (
        block_out,
        hidden_grad,
        shares[0],
        shares[1],
        shares[2],
        shares[3],
        shares[4],
        shares[5],
        expert_in_share,
        expert_down_share,
    )


def solution(mesh):
    placed = (
        P(("dp", "expert"), None),
        P(("dp", "expert")),
        P(("dp", "expert"), None),
        P(),
        P("dp"),
        P("dp", None),
        P("dp", None),
        P("dp", None),
        P("dp"),
        P("dp", None),
        P("expert", "dp", None),
        P("expert", "dp", None),
        P(("dp", "expert"), None),
    )
    return jax.shard_map(
        on_device,
        mesh=mesh,
        in_specs=placed,
        out_specs=(
            P(("dp", "expert"), None),
            P(("dp", "expert"), None),
            P("dp"),
            P("dp", None),
            P("dp", None),
            P("dp", None),
            P("dp"),
            P("dp", None),
            P("expert", "dp", None),
            P("expert", "dp", None),
        ),
        check_vma=False,
    )
```

profile of v0, /device:TPU:0, one launch (start us, length us, event | category | flops | bytes accessed | tf_op | source)
XLA Modules:
  0.0 1302.5 jit_solution(16895983580542270407)
XLA Ops:
  10.0 5.3 all-gather
  16.9 4.3 all-gather.1
  21.8 4.6 reduce-window.6
  27.9 15.5 %scatter_custom_fusion = s32[4097]{0:T(1024)S(1)} fusion(s32[4096]{0:T(1024)S(1)} %bitcast.208, s32[4096]{0:T(1024)S(1)} %add_select_fusion, s32[]{:T(128)} %constant.102.clone.1), kind=kCustom, calls=%fused_computation.144 | custom fusion | bytes 16392 | tf_op jit(solution)/shard_map/scatter | solution.py:163
  50.3 29.9 %all-gather.10.cloned.1.call-done = bf16[1024,1024]{1,0:T(8,128)(2,1)} async-done(((bf16[512,1024]{1,0:T(8,128)(2,1)}), bf16[1024,1024]{1,0:T(8,128)(2,1)}) %all-gather.10.cloned.1.call-update) | async-done | bytes 2097168 | tf_op jit(solution)/shard_map/all_gather | solution.py:87
  85.1 8.0 fusion.89
  94.7 8.4 exponential_reduce_fusion
  103.1 8.4 fusion.38
  119.9 18.2 %gather_fusion = bf16[4096,1024]{1,0:T(8,128)(2,1)} fusion(bf16[513,1024]{1,0:T(8,128)(2,1)S(1)} %concatenate.63, s32[4096]{0:T(1024)S(1)} %copy-done.36), kind=kCustom, calls=%fused_computation | custom fusion | bytes 16793600 | tf_op jit(solution)/shard_map/gather | solution.py:168
  138.0 5.7 all-to-all-start
  145.2 18.6 %gather_fusion.2 = f32[4096,1024]{1,0:T(8,128)} fusion(f32[513,1024]{1,0:T(8,128)S(1)} %concatenate.65, s32[4096]{0:T(1024)S(1)} %copy-done.36), kind=kCustom, calls=%fused_computation.2 | custom fusion | bytes 33570816 | tf_op jit(solution)/shard_map/gather | solution.py:216
  163.8 4.4 all_gather.31
  169.3 15.5 %scatter_custom_fusion.1 = f32[4097]{0:T(1024)S(1)} fusion(s32[4096]{0:T(1024)S(1)} %bitcast.209, f32[4096]{0:T(1024)S(1)} %get-tuple-element.77, f32[]{:T(128)} %constant.57.clone.1), kind=kCustom, calls=%fused_computation.142 | custom fusion | bytes 16392 | tf_op jit(solution)/shard_map/scatter | solution.py:212
  184.8 9.0 multiply_convert_fusion
  193.9 100.5 %all-to-all-done = bf16[16,256,1024]{2,1,0:T(8,128)(2,1)} async-done(((bf16[16,256,1024]{2,1,0:T(8,128)(2,1)}), bf16[16,256,1024]{2,1,0:T(8,128)(2,1)}, u32[]{:S(2)}, u32[]{:S(2)}) %all-to-all-start) | async-done | bytes 8388640 | tf_op jit(solution)/shard_map/all_to_all | solution.py:169
  294.4 36.5 %all-to-all-start.2 = ((bf16[16,256,1024]{2,1,0:T(8,128)(2,1)}), bf16[16,256,1024]{2,1,0:T(8,128)(2,1)}, u32[]{:S(2)}, u32[]{:S(2)}) async-start(bf16[16,256,1024]{2,1,0:T(8,128)(2,1)} %multiply_convert_fusion), calls=%async_computation.2 | async-start | bytes 16777216 | tf_op jit(solution)/shard_map/all_to_all | solution.py:221
  332.1 34.4 %all-gather.14.cloned.1.call-done = bf16[1,1024,1024]{2,1,0:T(8,128)(2,1)} async-done(((bf16[1,512,1024]{2,1,0:T(8,128)(2,1)}), bf16[1,1024,1024]{2,1,0:T(8,128)(2,1)}) %all-gather.14.cloned.1.call-update) | async-done | bytes 2097168 | tf_op jit(solution)/shard_map/all_gather | solution.py:94
  366.5 16.6 %convolution_bitcast_fusion = f32[16,1,256,1024]{3,2,0,1:T(8,128)} fusion(bf16[16,256,1024]{2,1,0:T(8,128)(2,1)} %all-to-all-done, bf16[1,1024,1024]{2,1,0:T(8,128)(2,1)} %all-gather.14.cloned.1.call-done), kind=kOutput, calls=%fused_computation.21 | convolution fusion | flops 8589934592 | bytes 27262976 | tf_op jit(solution)/shard_map/nlcd,ldf->nlcf/dot_general | solution.py:171
  383.1 6.1 all-gather.16.cloned.1.call-done
  389.2 92.4 %all-to-all-done.2 = bf16[16,256,1024]{2,1,0:T(8,128)(2,1)} async-done(((bf16[16,256,1024]{2,1,0:T(8,128)(2,1)}), bf16[16,256,1024]{2,1,0:T(8,128)(2,1)}, u32[]{:S(2)}, u32[]{:S(2)}) %all-to-all-start.2) | async-done | bytes 8388640 | tf_op jit(solution)/shard_map/all_to_all | solution.py:221
  481.6 15.6 %fusion.14 = (bf16[16,256,512]{2,1,0:T(8,128)(2,1)}, bf16[16,256,512]{2,1,0:T(8,128)(2,1)}, bf16[16,256,512]{2,1,0:T(8,128)(2,1)S(1)}) fusion(f32[16,1,256,1024]{3,2,0,1:T(8,128)} %convolution_bitcast_fusion, bf16[16,256,1024]{2,1,0:T(8,128)(2,1)} %all-to-all-done.2, bf16[1,1024,512]{2,1,0:T(8,128)(2,1)} %all-gather.16.cloned.1.call-done), kind=kOutput, calls=%fused_computation.38 | convolution fusion | flops 4326424576 | bytes 38797312 | tf_op jit(solution)/shard_map/nlcd,ldf->nlcf/dot_general | solution.py:226
  499.3 6.8 convolution_convert_fusion.1
  506.0 36.9 %all-to-all-start.1 = ((bf16[16,256,1024]{2,1,0:T(8,128)(2,1)}), bf16[16,256,1024]{2,1,0:T(8,128)(2,1)}, u32[]{:S(2)}, u32[]{:S(2)}) async-start(bf16[16,256,1024]{2,1,0:T(8,128)(2,1)} %convolution_convert_fusion.1), calls=%async_computation.1 | async-start | bytes 16777216 | tf_op jit(solution)/shard_map/all_to_all | solution.py:182
  542.9 14.7 %convolution_convert_fusion = bf16[16,256,1024]{2,1,0:T(8,128)(2,1)} fusion(bf16[16,256,512]{2,1,0:T(8,128)(2,1)} %get-tuple-element.80, bf16[16,256,512]{2,1,0:T(8,128)(2,1)} %get-tuple-element.79, bf16[1,1024,1024]{2,1,0:T(8,128)(2,1)S(1)} %copy-done.58), kind=kOutput, calls=%fused_computation.32 | convolution fusion | flops 8610906112 | bytes 18874368 | tf_op jit(solution)/shard_map/nlcf,ldf->nlcd/dot_general | solution.py:238
  557.7 135.9 %all-to-all-done.1 = bf16[16,256,1024]{2,1,0:T(8,128)(2,1)} async-done(((bf16[16,256,1024]{2,1,0:T(8,128)(2,1)}), bf16[16,256,1024]{2,1,0:T(8,128)(2,1)}, u32[]{:S(2)}, u32[]{:S(2)}) %all-to-all-start.1) | async-done | bytes 8388640 | tf_op jit(solution)/shard_map/all_to_all | solution.py:182
  693.6 36.5 %all-to-all-start.3 = ((bf16[16,256,1024]{2,1,0:T(8,128)(2,1)}), bf16[16,256,1024]{2,1,0:T(8,128)(2,1)}, u32[]{:S(2)}, u32[]{:S(2)}) async-start(bf16[16,256,1024]{2,1,0:T(8,128)(2,1)} %convolution_convert_fusion), calls=%async_computation.3 | async-start | bytes 16777216 | tf_op jit(solution)/shard_map/all_to_all | solution.py:241
  730.9 7.7 concatenate.64
  738.6 25.4 %gather_fusion.1 = bf16[4096,1024]{1,0:T(8,128)(2,1)} fusion(bf16[4097,1024]{1,0:T(8,128)(2,1)} %concatenate.64, s32[4096]{0:T(1024)S(1)} %broadcast_clamp_fusion), kind=kCustom, calls=%fused_computation.1 | custom fusion | bytes 16793600 | tf_op jit(solution)/shard_map/gather | solution.py:196
  763.9 10.0 fusion.1
  775.1 105.7 %all-to-all-done.3 = bf16[16,256,1024]{2,1,0:T(8,128)(2,1)} async-done(((bf16[16,256,1024]{2,1,0:T(8,128)(2,1)}), bf16[16,256,1024]{2,1,0:T(8,128)(2,1)}, u32[]{:S(2)}, u32[]{:S(2)}) %all-to-all-start.3) | async-done | bytes 8388640 | tf_op jit(solution)/shard_map/all_to_all | solution.py:241
  880.9 7.6 concatenate.69
  888.5 25.7 %gather_fusion.3 = bf16[4096,1024]{1,0:T(8,128)(2,1)} fusion(bf16[4097,1024]{1,0:T(8,128)(2,1)} %concatenate.69, s32[4096]{0:T(1024)S(1)} %broadcast_clamp_fusion), kind=kCustom, calls=%fused_computation.3 | custom fusion | bytes 16793600 | tf_op jit(solution)/shard_map/gather | solution.py:256
  914.2 12.0 convert_reduce_fusion
  934.2 14.2 %fusion.2 = (f32[8,2,512]{2,1,0:T(2,128)S(1)}, f32[8,512,512,2]{2,1,3,0:T(8,128)}) fusion(f32[8,2,512,512]{2,3,1,0:T(8,128)} %get-tuple-element.97, f32[8,2,512]{2,1,0:T(2,128)S(1)} %bitcast.199, bf16[512,8,64,1]{0,2,3,1:T(8,128)(2,1)S(1)} %bitcast.192, bf16[512,8,2,64]{0,3,2,1:T(8,128)(2,1)S(1)} %bitcast.185), kind=kOutput, calls=%fused_computation.13 | convolution fusion | flops 549445632 | bytes 35192832 | tf_op jit(solution)/shard_map/while/body/eval_jaxpr/qkgd,skd->kgqs/dot_general | solution.py:276
  948.4 8.6 fusion.45
  957.1 11.0 fusion.4
  968.1 6.0 broadcast_multiply_fusion
  979.9 4.9 convolution_multiply_fusion
  995.4 10.1 fusion.41
  1005.6 14.7 %fusion.37 = bf16[1,1024,1024]{2,1,0:T(8,128)(2,1)} fusion(bf16[16,256,1024]{2,1,0:T(8,128)(2,1)} %all-to-all-done, bf16[16,256,512]{2,1,0:T(8,128)(2,1)} %get-tuple-element.80, bf16[16,256,512]{2,1,0:T(8,128)(2,1)} %get-tuple-element.79), kind=kOutput, calls=%fused_computation.76 | convolution fusion | flops 8607760384 | bytes 18874368 | tf_op jit(solution)/shard_map/nlcd,nlcf->ldf/dot_general | solution.py:235
  1022.4 19.4 %reduce-scatter.13.cloned.1.call-done = bf16[512,1024]{1,0:T(8,128)(2,1)} async-done(((bf16[1024,1024]{1,0:T(8,128)(2,1)}), bf16[512,1024]{1,0:T(8,128)(2,1)}) %reduce-scatter.13.cloned.1.call-update) | async-done | bytes 1048592 | tf_op jit(solution)/shard_map/reduce_scatter | solution.py:350
  1041.8 34.8 %reduce-scatter.11.cloned.1.call-done = bf16[512,1024]{1,0:T(8,128)(2,1)} async-done(((bf16[1024,1024]{1,0:T(8,128)(2,1)}), bf16[512,1024]{1,0:T(8,128)(2,1)}) %reduce-scatter.11.cloned.1.call-update) | async-done | bytes 1048592 | tf_op jit(solution)/shard_map/reduce_scatter | solution.py:347
  1076.5 34.7 %reduce-scatter.15.cloned.1.call-done = bf16[512,1024]{1,0:T(8,128)(2,1)} async-done(((bf16[1024,1024]{1,0:T(8,128)(2,1)}), bf16[512,1024]{1,0:T(8,128)(2,1)}) %reduce-scatter.15.cloned.1.call-update) | async-done | bytes 1048592 | tf_op jit(solution)/shard_map/reduce_scatter | solution.py:353
  1112.5 22.0 %reduce-scatter.9.cloned.1.call-done = bf16[1,512,512]{2,1,0:T(8,128)(2,1)} async-done(((bf16[1,1024,512]{2,1,0:T(8,128)(2,1)}), bf16[1,512,512]{2,1,0:T(8,128)(2,1)}) %reduce-scatter.9.cloned.1.call-update) | async-done | bytes 524304 | tf_op jit(solution)/shard_map/reduce_scatter | solution.py:367
  1136.6 31.8 %reduce-scatter.7.cloned.1.call-done = bf16[1,512,1024]{2,1,0:T(8,128)(2,1)} async-done(((bf16[1,1024,1024]{2,1,0:T(8,128)(2,1)}), bf16[1,512,1024]{2,1,0:T(8,128)(2,1)}) %reduce-scatter.7.cloned.1.call-update) | async-done | bytes 1048592 | tf_op jit(solution)/shard_map/reduce_scatter | solution.py:364
  1176.3 4.9 all-reduce.8
  1185.2 61.1 %all-reduce.6 = (bf16[512]{0:T(512)(128)(2,1)S(1)}, bf16[512]{0:T(512)(128)(2,1)S(1)}, bf16[512,16]{0,1:T(8,128)(2,1)S(1)}) all-reduce(bf16[512]{0:T(512)(128)(2,1)S(1)} %dynamic-slice.2, bf16[512]{0:T(512)(128)(2,1)S(1)} %dynamic-slice.4, ...), channel_id=1, replica_groups=mesh['dp'=2,'expert'=16] {'expert'}, use_global_device_ids=true, to_apply=%region_22.23 | all-reduce | flops 9216 | bytes 36864 | tf_op jit(solution)/shard_map/psum | solution.py:336
  1248.0 41.4 %all-reduce.11.cloned.1.call-done = (bf16[512,1024]{1,0:T(8,128)(2,1)}, bf16[512,1024]{1,0:T(8,128)(2,1)}, bf16[512,1024]{1,0:T(8,128)(2,1)}) async-done(((bf16[512,1024]{1,0:T(8,128)(2,1)}, bf16[512,1024]{1,0:T(8,128)(2,1)}, bf16[512,1024]{1,0:T(8,128)(2,1)}), (bf16[512,1024]{1,0:T(8,128)(2,1)}, bf16[512,1024]{1,0:T(8,128)(2,1)}, bf16[512,1024]{1,0:T(8,128)(2,1)})) %all-reduce.11.cloned.1.call-update) | async-done | bytes 3145744 | tf_op jit(solution)/shard_map/psum | solution.py:337
  (251 shorter events, 83.9 us)
Async XLA Ops:
  7.2 38.2 %all-gather.8.cloned.1.call-start = ((), (), s32[]{:S(2)}) async-start(), calls=%async_computation.10 | async-start | bytes 3145728 | tf_op jit(solution)/shard_map/all_gather | solution.py:88
  7.9 8.7 copy-start.50
  8.0 72.2 %all-gather.10.cloned.1.call-start = ((), (), s32[]{:S(2)}) async-start(), calls=%async_computation.11 | async-start | bytes 3145728 | tf_op jit(solution)/shard_map/all_gather | solution.py:87
  8.7 8.1 copy-start.54
  8.7 106.1 %all-gather.12.cloned.1.call-start = ((), (), s32[]{:S(2)}) async-start(), calls=%async_computation.12 | async-start | bytes 3145728 | tf_op jit(solution)/shard_map/all_gather | solution.py:89
  9.9 17.6 %copy-start.55 = (s32[16]{0:T(128)S(1)}, s32[16]{0:T(128)}, u32[]{:S(2)}) copy-start(s32[16]{0:T(128)} %param.16) | copy-start | bytes 196
  15.2 30.2 %copy-start.47 = (f32[2,1,512]{2,1,0:T(1,128)}, f32[2,1,512]{2,1,0:T(1,128)S(1)}, u32[]{:S(2)}) copy-start(f32[2,1,512]{2,1,0:T(1,128)S(1)} %convert_element_type.227) | copy-start | bytes 12292
  15.5 32.8 %copy-start.51 = (f32[512]{0:T(512)}, f32[512]{0:T(512)S(1)}, u32[]{:S(2)}) copy-start(f32[512]{0:T(512)S(1)} %add_rsqrt_fusion.1) | copy-start | bytes 6148
  16.6 67.7 %copy-start.17 = (f32[512,64]{0,1:T(8,128)}, f32[512,64]{0,1:T(8,128)S(1)}, u32[]{:S(2)}) copy-start(f32[512,64]{0,1:T(8,128)S(1)} %get-tuple-element.94) | copy-start | bytes 393220
  27.8 20.5 %copy-start.37 = (s32[4096]{0:T(1024)}, s32[4096]{0:T(1024)S(1)}, u32[]{:S(2)}) copy-start(s32[4096]{0:T(1024)S(1)} %get-tuple-element.57) | copy-start | bytes 49156
  27.8 20.5 %copy-start.39 = (s32[4096]{0:T(1024)}, s32[4096]{0:T(1024)S(1)}, u32[]{:S(2)}) copy-start(s32[4096]{0:T(1024)S(1)} %get-tuple-element.68) | copy-start | bytes 49156
  27.9 20.5 %copy-start.41 = (s32[4096,1]{0,1:T(1,128)}, s32[4096,1]{0,1:T(1,128)S(1)}, u32[]{:S(2)}) copy-start(s32[4096,1]{0,1:T(1,128)S(1)} %compare_select_fusion) | copy-start | bytes 49156
  85.1 8.0 copy-start.2
  94.7 8.4 copy-start.13
  103.1 8.5 copy-start.26
  119.4 48.8 %copy-start.4 = (bf16[512,1024]{1,0:T(8,128)(2,1)}, bf16[512,1024]{1,0:T(8,128)(2,1)S(1)}, u32[]{:S(2)}) copy-start(bf16[512,1024]{1,0:T(8,128)(2,1)S(1)} %multiply_convert_fusion.2) | copy-start | bytes 3145732
  138.0 156.4 %all-to-all-start = ((bf16[16,256,1024]{2,1,0:T(8,128)(2,1)}), bf16[16,256,1024]{2,1,0:T(8,128)(2,1)}, u32[]{:S(2)}, u32[]{:S(2)}) async-start(bf16[16,256,1024]{2,1,0:T(8,128)(2,1)} %bitcast.184), calls=%async_computation | async-start | bytes 16777216 | tf_op jit(solution)/shard_map/all_to_all | solution.py:169
  145.2 18.6 %copy-start.49 = (bf16[512,16]{0,1:T(8,128)(2,1)S(1)}, bf16[512,16]{0,1:T(8,128)(2,1)}, u32[]{:S(2)}) copy-start(bf16[512,16]{0,1:T(8,128)(2,1)} %param.22) | copy-start | bytes 49156
  145.2 24.1 %copy-start.38 = (s32[4096]{0:T(1024)S(1)}, s32[4096]{0:T(1024)}, u32[]{:S(2)}) copy-start(s32[4096]{0:T(1024)} %copy-done.37) | copy-start | bytes 49156
  145.2 24.1 %copy-start.40 = (s32[4096]{0:T(1024)S(1)}, s32[4096]{0:T(1024)}, u32[]{:S(2)}) copy-start(s32[4096]{0:T(1024)} %copy-done.39) | copy-start | bytes 49156
  145.2 24.1 %copy-start.42 = (s32[4096,1]{0,1:T(1,128)S(1)}, s32[4096,1]{0,1:T(1,128)}, u32[]{:S(2)}) copy-start(s32[4096,1]{0,1:T(1,128)} %copy-done.41) | copy-start | bytes 49156
  294.4 187.3 %all-to-all-start.2 = ((bf16[16,256,1024]{2,1,0:T(8,128)(2,1)}), bf16[16,256,1024]{2,1,0:T(8,128)(2,1)}, u32[]{:S(2)}, u32[]{:S(2)}) async-start(bf16[16,256,1024]{2,1,0:T(8,128)(2,1)} %multiply_convert_fusion), calls=%async_computation.2 | async-start | bytes 16777216 | tf_op jit(solution)/shard_map/all_to_all | solution.py:221
  330.9 35.6 %all-gather.14.cloned.1.call-start = ((), (), s32[]{:S(2)}) async-start(), calls=%async_computation.13 | async-start | bytes 3145728 | tf_op jit(solution)/shard_map/all_gather | solution.py:94
  331.5 57.7 %all-gather.16.cloned.1.call-start = ((), (), s32[]{:S(2)}) async-start(), calls=%async_computation.14 | async-start | bytes 1572864 | tf_op jit(solution)/shard_map/all_gather | solution.py:95
  389.2 110.0 %copy-start.59 = (bf16[1,1024,512]{2,1,0:T(8,128)(2,1)S(1)}, bf16[1,1024,512]{2,1,0:T(8,128)(2,1)}, u32[]{:S(2)}) copy-start(bf16[1,1024,512]{2,1,0:T(8,128)(2,1)} %all-gather.16.cloned.1.call-done) | copy-start | bytes 3145732
  506.0 36.9 %copy-start.58 = (bf16[1,1024,1024]{2,1,0:T(8,128)(2,1)S(1)}, bf16[1,1024,1024]{2,1,0:T(8,128)(2,1)}, u32[]{:S(2)}) copy-start(bf16[1,1024,1024]{2,1,0:T(8,128)(2,1)} %all-gather.14.cloned.1.call-done) | copy-start | bytes 6291460
  506.0 187.5 %all-to-all-start.1 = ((bf16[16,256,1024]{2,1,0:T(8,128)(2,1)}), bf16[16,256,1024]{2,1,0:T(8,128)(2,1)}, u32[]{:S(2)}, u32[]{:S(2)}) async-start(bf16[16,256,1024]{2,1,0:T(8,128)(2,1)} %convolution_convert_fusion.1), calls=%async_computation.1 | async-start | bytes 16777216 | tf_op jit(solution)/shard_map/all_to_all | solution.py:182
  557.7 172.5 %copy-start.6 = (bf16[512,1024]{1,0:T(8,128)(2,1)S(1)}, bf16[512,1024]{1,0:T(8,128)(2,1)}, u32[]{:S(2)}) copy-start(bf16[512,1024]{1,0:T(8,128)(2,1)} %param.25) | copy-start | bytes 3145732
  693.6 187.3 %all-to-all-start.3 = ((bf16[16,256,1024]{2,1,0:T(8,128)(2,1)}), bf16[16,256,1024]{2,1,0:T(8,128)(2,1)}, u32[]{:S(2)}, u32[]{:S(2)}) async-start(bf16[16,256,1024]{2,1,0:T(8,128)(2,1)} %convolution_convert_fusion), calls=%async_computation.3 | async-start | bytes 16777216 | tf_op jit(solution)/shard_map/all_to_all | solution.py:241
  730.1 311.6 %reduce-scatter.13.cloned.1.call-start = ((), (), s32[]{:S(2)}) async-start(), calls=%async_computation.18 | async-start | bytes 3145728 | tf_op jit(solution)/shard_map/reduce_scatter | solution.py:350
  914.2 12.0 copy-start.1
  914.2 12.0 copy-start.34
  914.2 12.0 copy-start.44
  914.2 12.0 copy-start.46
  934.2 22.8 %slice-start = ((s8[16777216]{0:T(1024)(128)(4,1)}), s8[4194304]{0:T(1024)(128)(4,1)S(1)}, s32[]{:S(2)}) async-start(s8[16777216]{0:T(1024)(128)(4,1)} %bitcast.181), calls=%async_computation.22 | async-start | bytes 8388608
  934.2 22.8 %slice-start.1 = ((s8[16777216]{0:T(1024)(128)(4,1)}), s8[4194304]{0:T(1024)(128)(4,1)S(1)}, s32[]{:S(2)}) async-start(s8[16777216]{0:T(1024)(128)(4,1)} %bitcast.181), calls=%async_computation.23 | async-start | bytes 8388608
  934.2 22.8 %slice-start.2 = ((s8[16777216]{0:T(1024)(128)(4,1)}), s8[4194304]{0:T(1024)(128)(4,1)S(1)}, s32[]{:S(2)}) async-start(s8[16777216]{0:T(1024)(128)(4,1)} %bitcast.181), calls=%async_computation.24 | async-start | bytes 8388608
  948.4 8.7 slice-start.3
  957.0 18.3 %copy-start.28 = (bf16[8,64,512]{2,1,0:T(8,128)(2,1)}, bf16[8,64,512]{2,1,0:T(8,128)(2,1)S(1)}, u32[]{:S(2)}) copy-start(bf16[8,64,512]{2,1,0:T(8,128)(2,1)S(1)} %fusion.45) | copy-start | bytes 1572868
  957.1 11.0 copy-start.3
  957.1 11.0 copy-start.22
  978.9 97.6 %reduce-scatter.11.cloned.1.call-start = ((), (), s32[]{:S(2)}) async-start(), calls=%async_computation.17 | async-start | bytes 3145728 | tf_op jit(solution)/shard_map/reduce_scatter | solution.py:347
  989.8 121.4 %reduce-scatter.15.cloned.1.call-start = ((), (), s32[]{:S(2)}) async-start(), calls=%async_computation.19 | async-start | bytes 3145728 | tf_op jit(solution)/shard_map/reduce_scatter | solution.py:353
  995.2 139.3 %reduce-scatter.9.cloned.1.call-start = ((), (), s32[]{:S(2)}) async-start(), calls=%async_computation.16 | async-start | bytes 1572864 | tf_op jit(solution)/shard_map/reduce_scatter | solution.py:367
  1005.5 162.9 %reduce-scatter.7.cloned.1.call-start = ((), (), s32[]{:S(2)}) async-start(), calls=%async_computation.15 | async-start | bytes 3145728 | tf_op jit(solution)/shard_map/reduce_scatter | solution.py:364
  1020.3 91.0 %copy-start.60 = (u32[32]{0:T(128)S(1)}, u32[32]{0:T(128)}, u32[]{:S(2)}) copy-start(u32[32]{0:T(128)} %constant.126) | copy-start | bytes 388
  1020.3 164.9 %reduce-scatter.17.cloned.1.call-start = ((), (), s32[]{:S(2)}) async-start(), calls=%async_computation.20 | async-start | bytes 49152 | tf_op jit(solution)/shard_map/reduce_scatter | solution.py:359
  1022.4 267.1 %all-reduce.11.cloned.1.call-start = ((), (), s32[]{:S(2)}) async-start(), calls=%async_computation.21 | async-start | bytes 6291456 | tf_op jit(solution)/shard_map/psum | solution.py:337
  (34 other events, 71.8 us)
Sparse Core Ops, SparseCore 0:
  9.6 35.8 all-gather.7
  47.0 33.1 all-gather.9
  81.7 33.1 all-gather.11
  333.0 33.4 all-gather.13
  367.9 21.2 all-gather.15
  979.0 62.6 reduce-scatter.12
  1044.7 31.8 reduce-scatter.10
  1079.3 31.8 reduce-scatter.14
  1114.1 20.3 reduce-scatter.8
  1136.6 31.8 reduce-scatter.6
  1171.3 9.8 reduce-scatter.16
  1185.4 103.9 all-reduce.10
where the time goes:
time: 1310 us; the launch traced here: 1300 us
  waiting for transfers between devices  697 us (53%)
  matrix products  157 us (12%)
  local copies, waits for them, and re-layouts  156 us (12%)
  starting transfers between devices  116 us (9%)
  other arithmetic  80.7 us (6%)
  blocking collectives  80 us (6%)
  between operations  16.2 us (1%)
    all_to_all x1, waiting for transfers between devices, on_device(): lax.all_to_all(expert_out.reshape(owners, local_count * capacity, model_w...  136 us
    all_to_all x1, waiting for transfers between devices, on_device(): lax.all_to_all(row_grads.reshape(owners, local_count * capacity, model_wi...  106 us
    all_to_all x1, waiting for transfers between devices, on_device(): lax.all_to_all(outgoing, 'expert', split_axis=0, concat_axis=0, tiled=True)  101 us
    all_to_all x1, waiting for transfers between devices, on_device(): lax.all_to_all(out_grads, 'expert', split_axis=0, concat_axis=0, tiled=True)  92.4 us
    psum x1, blocking collectives, on_device(): lax.psum(dense_parts[0].astype(jnp.bfloat16), 'expert').astype(jnp.float32)  61.1 us
    psum x1, waiting for transfers between devices, on_device(): lax.psum(dense_parts[1].astype(jnp.bfloat16), 'expert').astype(jnp.float32)  41.4 us
    all_to_all x1, starting transfers between devices, on_device(): lax.all_to_all(expert_out.reshape(owners, local_count * capacity, model_w...  36.9 us
    all_to_all x1, starting transfers between devices, on_device(): lax.all_to_all(out_grads, 'expert', split_axis=0, concat_axis=0, tiled=True)  36.5 us
  transfers between devices with their start and end apart: 16, of which 15 were waited for; matrix products, arithmetic and copies ran while one was open for 18% of the time, Pallas kernels for 0%

commit v1 on v0

v1 whole, which is shorter than its diff:
```python
import jax
import jax.numpy as jnp
from jax import lax
from jax.sharding import PartitionSpec as P

QUERY_HEADS = 16
KEY_VALUE_HEADS = 8
HEAD_DIMENSION = 64
FF = 512
BLOCK_ROWS = 128
CB = 2


norm_eps = 1e-06
theta_base = 10000.0


def rotary_tables(sequence_length, head_dim):
    half_dim = head_dim // 2
    inverse = theta_base ** (-jnp.arange(half_dim, dtype=jnp.float32) * 2.0 / head_dim)
    angles = jnp.arange(sequence_length, dtype=jnp.float32)[:, None] * inverse[None, :]
    angles = jnp.concatenate([angles, angles], axis=-1)
    return (jnp.cos(angles), jnp.sin(angles))


def apply_rotation(value, cosine_lookup, sine_lookup):
    half_dim = value.shape[-1] // 2
    turned = jnp.concatenate([-value[..., half_dim:], value[..., :half_dim]], axis=-1)
    return value * cosine_lookup[:, None, :] + turned * sine_lookup[:, None, :]


def unrotate(grad_val, cosine_lookup, sine_lookup):
    half_dim = grad_val.shape[-1] // 2
    scaled = grad_val * sine_lookup[:, None, :]
    turned = jnp.concatenate([scaled[..., half_dim:], -scaled[..., :half_dim]], axis=-1)
    return grad_val * cosine_lookup[:, None, :] + turned


def masked_scores(query_block, key_rot, block_start, seg_ids, scale):
    span_len = query_block.shape[0]
    raw_scores = (
        jnp.einsum("qkgd,skd->kgqs", query_block, key_rot, preferred_element_type=jnp.float32)
        * scale
    )
    query_pos = block_start + jnp.arange(span_len, dtype=jnp.int32)
    key_pos = jnp.arange(key_rot.shape[0], dtype=jnp.int32)
    allowed = (query_pos[:, None] >= key_pos[None, :]) & (seg_ids[:, None] == seg_ids[None, :])
    return jnp.where(allowed[None, None], raw_scores, -1e30)


def norm_backward(grad_in, gain_vec, normalized, inverse_rms):
    scaled = grad_in * gain_vec
    return inverse_rms * (
        scaled - normalized * jnp.mean(scaled * normalized, axis=-1, keepdims=True)
    )


def at_offset(arr, owners, dz, dx, dc):
    pairs = []
    for i in range(owners):
        z, x, c = i // 4, (i // 2) % 2, i % 2
        source = (((z + dz) % (owners // 4)) * 2 + (x ^ dx)) * 2 + (c ^ dc)
        pairs.append((source, i))
    return lax.ppermute(arr, "expert", pairs)


def swap_dp(arr):
    return lax.ppermute(arr, "dp", [(0, 1), (1, 0)])


def piece(arr, index, size, axis=0):
    return lax.dynamic_slice_in_dim(arr, index * size, size, axis)


def in_order(first, mine, other, axis=0):
    return jnp.where(
        first, jnp.concatenate([mine, other], axis), jnp.concatenate([other, mine], axis)
    )


def add_low(left, right):
    return (left.astype(jnp.float32) + right.astype(jnp.float32)).astype(jnp.bfloat16)


def gather_rows(arr, owners):
    across = owners // 4
    got = {(0, 0, 0): arr}
    got[0, 1, 0] = at_offset(arr, owners, 0, 1, 0)
    order = sorted(range(1, across), key=lambda k: min(k, across - k))
    for k in order:
        got[k, 0, 0] = at_offset(arr, owners, k, 0, 0)
    for k in order:
        got[k, 1, 0] = at_offset(got[k, 0, 0], owners, 0, 1, 0)
    for k in [0] + order:
        for x in range(2):
            got[k, x, 1] = at_offset(got[k, x, 0], owners, 0, 0, 1)
    return got


def scatter_rows(parts, owners):
    across = owners // 4
    order = sorted(range(1, across), key=lambda k: min(k, across - k))
    total = None
    for k in order + [0]:
        far = add_low(parts[k, 1, 0], at_offset(parts[k, 1, 1], owners, 0, 0, 1))
        near = add_low(parts[k, 0, 0], at_offset(parts[k, 0, 1], owners, 0, 0, 1))
        row = add_low(near, at_offset(far, owners, 0, 1, 0))
        if k:
            row = at_offset(row, owners, across - k, 0, 0)
        row = row.astype(jnp.float32)
        total = row if total is None else total + row
    return total


def whole_rows(arr, owners):
    if lax.axis_size("dp") != 2:
        return lax.all_gather(arr, "dp", axis=0, tiled=True)
    core = lax.axis_index("expert") % 2
    got = swap_dp(piece(arr, core, arr.shape[0] // 2))
    other = in_order(core == 0, got, at_offset(got, owners, 0, 0, 1))
    return in_order(lax.axis_index("dp") == 0, arr, other)


def whole_expert(arr):
    if lax.axis_size("dp") != 2:
        return lax.all_gather(arr, "dp", axis=0, tiled=True)
    return in_order(lax.axis_index("dp") == 0, arr, swap_dp(arr))


def fold_expert(grad):
    if lax.axis_size("dp") != 2:
        return lax.psum_scatter(
            grad.astype(jnp.bfloat16), "dp", scatter_dimension=0, tiled=True
        ).astype(jnp.float32)
    side = lax.axis_index("dp")
    half = grad.shape[0] // 2
    sent = swap_dp(piece(grad, 1 - side, half).astype(jnp.bfloat16))
    return piece(grad, side, half) + sent.astype(jnp.float32)


def fold_shared(grad, owners):
    low = grad.astype(jnp.bfloat16)
    if lax.axis_size("dp") != 2:
        return lax.psum_scatter(
            lax.psum(low, "expert"), "dp", scatter_dimension=0, tiled=True
        ).astype(jnp.float32)
    me = lax.axis_index("expert")
    z, x, c = me // 4, (me // 2) % 2, me % 2
    side = lax.axis_index("dp")
    across = owners // 4
    wide = low.shape[1] // 2
    low = add_low(
        piece(low, c, wide, 1), at_offset(piece(low, 1 - c, wide, 1), owners, 0, 0, 1)
    )
    half = low.shape[0] // 2
    low = add_low(piece(low, side, half), swap_dp(piece(low, 1 - side, half)))
    quarter = half // 2
    low = add_low(piece(low, x, quarter), at_offset(piece(low, 1 - x, quarter), owners, 0, 1, 0))
    rows = quarter // across
    total = piece(low, z, rows).astype(jnp.float32)
    for k in range(1, across):
        sent = at_offset(piece(low, (z + across - k) % across, rows), owners, k, 0, 0)
        total = total + sent.astype(jnp.float32)
    low = total.astype(jnp.bfloat16)
    turned = [low] + [at_offset(low, owners, k, 0, 0) for k in range(1, across)]
    low = lax.dynamic_slice_in_dim(
        jnp.concatenate(turned + turned, 0), ((across - z) % across) * rows, quarter, 0
    )
    low = in_order(x == 0, low, at_offset(low, owners, 0, 1, 0))
    low = in_order(c == 0, low, at_offset(low, owners, 0, 0, 1), 1)
    return low.astype(jnp.float32)


def on_device(
    hidden,
    segments,
    routes,
    capacity_blocks,
    attn_gain,
    w_query,
    key_value_weight,
    w_out,
    ffn_gain,
    w_router,
    expert_in,
    expert_down,
    cotangent,
):
    sequence_length = hidden.shape[0]
    model_width = hidden.shape[1]
    expert_count = capacity_blocks.shape[0]
    owners = lax.axis_size("expert")
    across = owners // 4
    capacity = BLOCK_ROWS * CB
    group_length = QUERY_HEADS // KEY_VALUE_HEADS
    key_columns = KEY_VALUE_HEADS * HEAD_DIMENSION
    scale = HEAD_DIMENSION ** (-0.5)
    brain_float_half = jnp.bfloat16
    single_float = jnp.float32
    small = lax.all_gather(
        jnp.concatenate([attn_gain[None], ffn_gain[None], w_router.T], axis=0),
        "dp",
        axis=1,
        tiled=True,
    )
    gain_attn = small[0].astype(single_float)
    gain_ffn = small[1].astype(single_float)
    full_router = small[2:].T
    full_query = whole_rows(w_query, owners)
    full_keyval = whole_rows(key_value_weight, owners)
    full_out = whole_rows(w_out, owners)
    expert_ids = jnp.arange(expert_count, dtype=jnp.int32)
    routed = jnp.any(routes[:, :, None] == expert_ids[None, None, :], axis=1)
    earlier = (
        jnp.arange(sequence_length)[:, None] > jnp.arange(sequence_length)[None, :]
    ).astype(brain_float_half)
    ranks = jnp.dot(
        earlier, routed.astype(brain_float_half), preferred_element_type=single_float
    )
    kept_mask = routed & (ranks < (BLOCK_ROWS * capacity_blocks[None, :]).astype(single_float))
    slots = jnp.where(kept_mask, ranks, -1.0)
    me = lax.axis_index("expert")
    offsets = [(k, x, c) for k in range(across) for x in range(2) for c in range(2)]
    sources = jnp.stack(
        [(((me // 4 + k) % across) * 2 + ((me // 2) % 2 ^ x)) * 2 + (me % 2 ^ c) for k, x, c in offsets]
    )

    def to_owners(columns):
        return lax.all_to_all(columns.T, "expert", split_axis=0, concat_axis=0, tiled=True)[sources]

    slots_here = to_owners(slots)
    select = {
        offset: (
            jnp.arange(capacity, dtype=jnp.int32)[:, None].astype(single_float)
            == slots_here[n][None, :]
        )
        for n, offset in enumerate(offsets)
    }
    cot_rows = gather_rows(cotangent, owners)
    full_in = whole_expert(expert_in[0])
    full_down = whole_expert(expert_down[0])
    resid_in = hidden.astype(single_float)
    inverse_one = lax.rsqrt(jnp.mean(resid_in * resid_in, axis=-1, keepdims=True) + norm_eps)
    normal_one = resid_in * inverse_one
    normed = (normal_one * gain_attn).astype(brain_float_half)
    query_pre = jnp.dot(normed, full_query, preferred_element_type=single_float)
    key_value_projected = jnp.dot(normed, full_keyval, preferred_element_type=single_float)
    cosine_lookup, sine_lookup = rotary_tables(sequence_length, HEAD_DIMENSION)
    query_rotated = apply_rotation(
        query_pre.reshape(sequence_length, QUERY_HEADS, HEAD_DIMENSION), cosine_lookup, sine_lookup
    ).astype(brain_float_half)
    key_rot = apply_rotation(
        key_value_projected[:, :key_columns].reshape(
            sequence_length, KEY_VALUE_HEADS, HEAD_DIMENSION
        ),
        cosine_lookup,
        sine_lookup,
    ).astype(brain_float_half)
    value_row_list = (
        key_value_projected[:, key_columns:]
        .reshape(sequence_length, KEY_VALUE_HEADS, HEAD_DIMENSION)
        .astype(brain_float_half)
    )
    block_length = min(512, sequence_length)
    block_total = sequence_length // block_length
    query_block_list = query_rotated.reshape(
        block_total, block_length, KEY_VALUE_HEADS, group_length, HEAD_DIMENSION
    )
    block_starts = jnp.arange(block_total, dtype=jnp.int32) * block_length

    def forward_block(pieces):
        query_block, block_start = pieces
        masked = masked_scores(query_block, key_rot, block_start, segments, scale)
        top_score = jnp.max(masked, axis=-1, keepdims=True)
        log_total = top_score + jnp.log(
            jnp.sum(jnp.exp(masked - top_score), axis=-1, keepdims=True)
        )
        prob_low = jnp.exp(masked - log_total).astype(brain_float_half)
        mixed = jnp.einsum(
            "kgqs,skd->qkgd", prob_low, value_row_list, preferred_element_type=single_float
        )
        return (mixed.astype(brain_float_half), log_total)

    attended_blocks, log_totals = lax.map(forward_block, (query_block_list, block_starts))
    attended = attended_blocks.reshape(sequence_length, QUERY_HEADS * HEAD_DIMENSION)
    first_sum = resid_in + jnp.dot(attended, full_out, preferred_element_type=single_float)
    inverse_two = lax.rsqrt(jnp.mean(first_sum * first_sum, axis=-1, keepdims=True) + norm_eps)
    normal_two = first_sum * inverse_two
    moe_in = (normal_two * gain_ffn).astype(brain_float_half)
    moe_rows = gather_rows(moe_in, owners)
    logits = jnp.dot(moe_in, full_router, preferred_element_type=single_float)
    gates = jax.nn.softmax(jnp.where(routed, logits, -jnp.inf), axis=-1)
    kept_gates = jnp.where(kept_mask, gates, 0.0)
    gates_here = to_owners(kept_gates)
    near_first = sorted(range(across), key=lambda k: min(k, across - k))
    split = max(1, across // 2)
    groups = [
        [(k, x, c) for k in part for x in range(2) for c in range(2)]
        for part in (near_first[:split], near_first[split:])
        if part
    ]
    out_parts, grad_parts, gate_parts = ({}, {}, {})
    in_part, down_part = (0.0, 0.0)
    for group in groups:
        pick = lambda rows: jnp.concatenate(
            [
                jnp.dot(
                    select[o].astype(brain_float_half), rows[o], preferred_element_type=single_float
                ).astype(brain_float_half)
                for o in group
            ],
            axis=0,
        )
        cot_here = pick(cot_rows)
        inputs_here = pick(moe_rows)
        slot_gate = jnp.concatenate(
            [
                jnp.sum(jnp.where(select[o], gates_here[offsets.index(o)][None, :], 0.0), axis=1)
                for o in group
            ]
        )[:, None]
        gate_up = jnp.dot(inputs_here, full_in, preferred_element_type=single_float)
        gate_part = gate_up[:, :FF]
        up_part = gate_up[:, FF:]
        sigmoid_g = jax.nn.sigmoid(gate_part)
        silu_g = gate_part * sigmoid_g
        expert_hidden = (silu_g * up_part).astype(brain_float_half)
        expert_out = jnp.einsum(
            "cf,df->cd", expert_hidden, full_down, preferred_element_type=single_float
        ).astype(brain_float_half)
        cot_single = cot_here.astype(single_float)
        slot_grad = jnp.sum(cot_single * expert_out.astype(single_float), axis=1)
        scaled_out = (expert_out.astype(single_float) * slot_gate).astype(brain_float_half)
        grad_rows = (cot_single * slot_gate).astype(brain_float_half)
        hidden_delta = jnp.dot(grad_rows, full_down, preferred_element_type=single_float)
        gate_delta = hidden_delta * up_part * sigmoid_g * (1.0 + gate_part * (1.0 - sigmoid_g))
        up_delta = hidden_delta * silu_g
        gate_up_grad = jnp.concatenate([gate_delta, up_delta], axis=-1).astype(brain_float_half)
        row_grads = jnp.einsum(
            "cf,df->cd", gate_up_grad, full_in, preferred_element_type=single_float
        ).astype(brain_float_half)
        down_part = down_part + jnp.einsum(
            "cd,cf->df", grad_rows, expert_hidden, preferred_element_type=single_float
        )
        in_part = in_part + jnp.einsum(
            "cd,cf->df", inputs_here, gate_up_grad, preferred_element_type=single_float
        )
        for n, o in enumerate(group):
            low = select[o].astype(brain_float_half)
            span = slice(n * capacity, (n + 1) * capacity)
            grad_parts[o] = jnp.einsum(
                "ct,cd->td", low, row_grads[span], preferred_element_type=single_float
            ).astype(brain_float_half)
            out_parts[o] = jnp.einsum(
                "ct,cd->td", low, scaled_out[span], preferred_element_type=single_float
            ).astype(brain_float_half)
            gate_parts[o] = jnp.sum(jnp.where(select[o], slot_grad[span][:, None], 0.0), axis=0)
    returned_gates = jnp.zeros((owners, sequence_length), single_float).at[sources].set(
        jnp.stack([gate_parts[o] for o in offsets]), unique_indices=True
    )
    gate_grad = lax.all_to_all(returned_gates, "expert", split_axis=0, concat_axis=0, tiled=True).T
    cot_value = cotangent.astype(single_float)
    select_grad = gates * (gate_grad - jnp.sum(gates * gate_grad, axis=-1, keepdims=True))
    logit_grad = select_grad.astype(brain_float_half)
    router_part = jnp.einsum("sd,se->ed", moe_in, logit_grad, preferred_element_type=single_float)
    moe_grad = jnp.einsum("se,de->sd", logit_grad, full_router, preferred_element_type=single_float)
    moe_grad = moe_grad + scatter_rows(grad_parts, owners)
    block_out = (first_sum + scatter_rows(out_parts, owners)).astype(brain_float_half)
    expert_in_share = fold_expert(in_part)[None]
    expert_down_share = fold_expert(down_part)[None]
    ffn_gain_part = jnp.sum(moe_grad * normal_two, axis=0)
    first_grad = cot_value + norm_backward(moe_grad, gain_ffn, normal_two, inverse_two)
    branch_grad = first_grad.astype(brain_float_half)
    out_part = jnp.einsum("sa,sd->ad", attended, branch_grad, preferred_element_type=single_float)
    attended_gradient = jnp.einsum(
        "sd,ad->sa", branch_grad, full_out, preferred_element_type=single_float
    ).astype(brain_float_half)
    gradient_blocks = attended_gradient.reshape(
        block_total, block_length, KEY_VALUE_HEADS, group_length, HEAD_DIMENSION
    )

    def backward_block(carry, pieces):
        key_acc, value_acc = carry
        query_block, grad_block, log_total, block_start = pieces
        masked = masked_scores(query_block, key_rot, block_start, segments, scale)
        probability = jnp.exp(masked - log_total)
        prob_low = probability.astype(brain_float_half)
        prob_grad = jnp.einsum(
            "qkgd,skd->kgqs", grad_block, value_row_list, preferred_element_type=single_float
        )
        row_dot = jnp.sum(probability * prob_grad, axis=-1, keepdims=True)
        score_grad = (probability * (prob_grad - row_dot)).astype(brain_float_half)
        query_delta = (
            jnp.einsum("kgqs,skd->qkgd", score_grad, key_rot, preferred_element_type=single_float)
            * scale
        )
        key_acc = (
            key_acc
            + jnp.einsum(
                "kgqs,qkgd->skd", score_grad, query_block, preferred_element_type=single_float
            )
            * scale
        )
        value_acc = value_acc + jnp.einsum(
            "kgqs,qkgd->skd", prob_low, grad_block, preferred_element_type=single_float
        )
        return ((key_acc, value_acc), query_delta)

    zeroed_rows = jnp.zeros((sequence_length, KEY_VALUE_HEADS, HEAD_DIMENSION), single_float)
    (key_delta, value_delta), query_deltas = lax.scan(
        backward_block,
        (zeroed_rows, zeroed_rows),
        (query_block_list, gradient_blocks, log_totals, block_starts),
    )
    query_grad_low = (
        unrotate(
            query_deltas.reshape(sequence_length, QUERY_HEADS, HEAD_DIMENSION),
            cosine_lookup,
            sine_lookup,
        )
        .astype(brain_float_half)
        .reshape(sequence_length, QUERY_HEADS * HEAD_DIMENSION)
    )
    key_grad_low = unrotate(key_delta, cosine_lookup, sine_lookup).reshape(
        sequence_length, key_columns
    )
    keyval_grad_low = jnp.concatenate(
        [key_grad_low, value_delta.reshape(sequence_length, key_columns)], axis=-1
    ).astype(brain_float_half)
    query_part = jnp.einsum(
        "sd,sa->da", normed, query_grad_low, preferred_element_type=single_float
    )
    keyval_part = jnp.einsum(
        "sd,sa->da", normed, keyval_grad_low, preferred_element_type=single_float
    )
    normed_grad = jnp.einsum(
        "sa,da->sd", query_grad_low, full_query, preferred_element_type=single_float
    )
    normed_grad = normed_grad + jnp.einsum(
        "sa,da->sd", keyval_grad_low, full_keyval, preferred_element_type=single_float
    )
    attn_gain_part = jnp.sum(normed_grad * normal_one, axis=0)
    hidden_grad = (
        first_grad + norm_backward(normed_grad, gain_attn, normal_one, inverse_one)
    ).astype(brain_float_half)
    side = lax.axis_index("dp")
    own = model_width // lax.axis_size("dp")
    early = lax.psum(
        jnp.concatenate([ffn_gain_part[None], router_part], axis=0), ("dp", "expert")
    )
    early = lax.dynamic_slice_in_dim(early, side * own, own, 1)
    late = lax.dynamic_slice_in_dim(lax.psum(attn_gain_part, ("dp", "expert")), side * own, own, 0)
    return (
        block_out,
        hidden_grad,
        late,
        fold_shared(query_part, owners),
        fold_shared(keyval_part, owners),
        fold_shared(out_part, owners),
        early[0],
        early[1:].T,
        expert_in_share,
        expert_down_share,
    )


def solution(mesh):
    placed = (
        P(("dp", "expert"), None),
        P(("dp", "expert")),
        P(("dp", "expert"), None),
        P(),
        P("dp"),
        P("dp", None),
        P("dp", None),
        P("dp", None),
        P("dp"),
        P("dp", None),
        P("expert", "dp", None),
        P("expert", "dp", None),
        P(("dp", "expert"), None),
    )
    return jax.shard_map(
        on_device,
        mesh=mesh,
        in_specs=placed,
        out_specs=(
            P(("dp", "expert"), None),
            P(("dp", "expert"), None),
            P("dp"),
            P("dp", None),
            P("dp", None),
            P("dp", None),
            P("dp"),
            P("dp", None),
            P("expert", "dp", None),
            P("expert", "dp", None),
        ),
        check_vma=False,
    )
```

time: 1310 us -> 946 us (0.72)
  waiting for transfers between devices: 697 us -> 446 us
  local copies, waits for them, and re-layouts: 156 us -> 33.9 us
  matrix products: 157 us -> 198 us
  blocking collectives: 80 us -> 60 us
  other arithmetic: 80.7 us -> 67.4 us
    ppermute x0 -> x103, waiting for transfers between devices: none -> 421 us  [the longest x93 377 us: at_offset(): return lax.ppermute(arr, 'expert', pairs)]
    all_to_all x4 -> x3, waiting for transfers between devices: 435 us -> 24.6 us  [the longest x2 22.5 us: to_owners(): lax.all_to_all(columns.T, 'expert', split_axis=0, concat_axis=0, tiled=True)]
    reduce_scatter x6 -> x0, waiting for transfers between devices: 143 us -> none  [the longest x1 34.8 us: on_device(): lax.psum_scatter(summed[1].astype(jnp.bfloat16), 'dp', scatter_dimension=...]
    all_to_all x4 -> x3, starting transfers between devices: 116 us -> 12.3 us  [the longest x2 8.8 us: to_owners(): lax.all_to_all(columns.T, 'expert', split_axis=0, concat_axis=0, tiled=True)]
    ppermute x0 -> x103, starting transfers between devices: none -> 103 us  [the longest x93 91.6 us: at_offset(): return lax.ppermute(arr, 'expert', pairs)]
    gather x4 -> x2, local copies, waits for them, and re-layouts: 87.8 us -> 1.39 us  [to_owners(): lax.all_to_all(columns.T, 'expert', split_axis=0, concat_axis=0, tiled=True)]
    all_gather x5 -> x0, waiting for transfers between devices: 75.1 us -> none  [the longest x1 34.4 us: on_device(): lax.all_gather(expert_in, 'dp', axis=1, tiled=True)]
    dot_general x7 -> x78, matrix products: 79.4 us -> 142 us  [the longest x32 30.3 us: on_device(): jnp.dot(select[o].astype(brain_float_half), rows[o], preferred_element_ty...]
  transfers between devices with their start and end apart: 16 -> 107, of which waited for: 15 -> 37; matrix products, arithmetic and copies ran while one was open for 18% -> 18% of each run, Pallas kernels for 0% -> 0%
where the time goes in v1:
time: 946 us; the launch traced here: 938 us
  waiting for transfers between devices  446 us (47%)
  matrix products  198 us (21%)
  starting transfers between devices  116 us (12%)
  other arithmetic  67.4 us (7%)
  blocking collectives  60 us (6%)
  local copies, waits for them, and re-layouts  33.9 us (4%)
  between operations  17.1 us (2%)
    ppermute x93, waiting for transfers between devices, at_offset(): return lax.ppermute(arr, 'expert', pairs)  377 us
    ppermute x93, starting transfers between devices, at_offset(): return lax.ppermute(arr, 'expert', pairs)  91.6 us
    ppermute x10, waiting for transfers between devices, swap_dp(): return lax.ppermute(arr, 'dp', [(0, 1), (1, 0)])  43.7 us
    psum x1, blocking collectives, on_device(): lax.psum(attn_gain_part, ('dp', 'expert'))  37.9 us
    dot_general x32, matrix products, on_device(): jnp.dot(select[o].astype(brain_float_half), rows[o], preferred_element_ty...  30.3 us
    all_to_all x2, waiting for transfers between devices, to_owners(): lax.all_to_all(columns.T, 'expert', split_axis=0, concat_axis=0, tiled=True)  22.5 us
    all_gather x1, blocking collectives, on_device(): lax.all_gather(jnp.concatenate([attn_gain[None], ffn_gain[None], w_router...  22.1 us
    dot_general x16, matrix products, on_device(): jnp.einsum('ct,cd->td', low, row_grads[span], preferred_element_type=sing...  21.4 us
  transfers between devices with their start and end apart: 107, of which 37 were waited for; matrix products, arithmetic and copies ran while one was open for 18% of the time, Pallas kernels for 0%

profile of v1, /device:TPU:0, one launch (start us, length us, event | category | flops | bytes accessed | tf_op | source)
XLA Modules:
  0.0 938.5 jit_solution(12097018108653981968)
XLA Ops:
  10.3 3.6 collective-permute-start.41
  18.4 22.1 %all_gather.3 = bf16[18,1024]{1,0:T(8,128)(2,1)S(1)} all-gather(bf16[18,512]{1,0:T(8,128)(2,1)S(1)} %pad_maximum_fusion.14), channel_id=1, replica_groups=mesh['dp'=2,'expert'=16] {'dp'}, dimensions={1}, use_global_device_ids=true | all-gather | bytes 55296 | tf_op jit(solution)/shard_map/all_gather | solution.py:200
  50.1 9.1 collective-permute-done.4
  70.0 7.5 fusion.385
  77.6 8.3 exponential_reduce_fusion
  85.9 8.5 fusion.46
  101.3 5.3 all-to-all-start
  109.2 4.2 all-to-all-done
  117.7 18.3 %all-to-all-done.1 = f32[16,1,512]{2,1,0:T(1,128)S(1)} async-done(((f32[16,1,512]{2,1,0:T(1,128)}), f32[16,1,512]{2,1,0:T(1,128)S(1)}, u32[]{:S(2)}, u32[]{:S(2)}) %all-to-all-start.1) | async-done | bytes 32800 | tf_op jit(solution)/shard_map/all_to_all | solution.py:229
  150.6 16.6 %collective-permute-done.7 = bf16[512,1024]{1,0:T(8,128)(2,1)S(1)} collective-permute-done((bf16[512,1024]{1,0:T(8,128)(2,1)S(1)}, bf16[512,1024]{1,0:T(8,128)(2,1)S(1)}, u32[]{:S(2)}, u32[]{:S(2)}) %collective-permute-start.7) | collective-permute-done | bytes 1048608 | tf_op jit(solution)/shard_map/ppermute | solution.py:64
  172.3 17.4 %collective-permute-done.43 = bf16[512,1024]{1,0:T(8,128)(2,1)S(1)} collective-permute-done((bf16[512,1024]{1,0:T(8,128)(2,1)}, bf16[512,1024]{1,0:T(8,128)(2,1)S(1)}, u32[]{:S(2)}, u32[]{:S(2)}) %collective-permute-start.43) | collective-permute-done | bytes 1048608 | tf_op jit(solution)/shard_map/ppermute | solution.py:64
  191.6 20.6 %collective-permute-done.47 = bf16[512,1024]{1,0:T(8,128)(2,1)S(1)} collective-permute-done((bf16[512,1024]{1,0:T(8,128)(2,1)}, bf16[512,1024]{1,0:T(8,128)(2,1)S(1)}, u32[]{:S(2)}, u32[]{:S(2)}) %collective-permute-start.47) | collective-permute-done | bytes 1048608 | tf_op jit(solution)/shard_map/ppermute | solution.py:64
  214.4 6.4 collective-permute-done.49
  222.2 12.4 %collective-permute-done.11 = bf16[512,1024]{1,0:T(8,128)(2,1)S(1)} collective-permute-done((bf16[512,1024]{1,0:T(8,128)(2,1)S(1)}, bf16[512,1024]{1,0:T(8,128)(2,1)S(1)}, u32[]{:S(2)}, u32[]{:S(2)}) %collective-permute-start.11) | collective-permute-done | bytes 1048608 | tf_op jit(solution)/shard_map/ppermute | solution.py:64
  237.5 19.6 %collective-permute-done.21 = bf16[512,1024]{1,0:T(8,128)(2,1)S(1)} collective-permute-done((bf16[512,1024]{1,0:T(8,128)(2,1)S(1)}, bf16[512,1024]{1,0:T(8,128)(2,1)S(1)}, u32[]{:S(2)}, u32[]{:S(2)}) %collective-permute-start.21) | collective-permute-done | bytes 1048608 | tf_op jit(solution)/shard_map/ppermute | solution.py:64
  259.9 8.0 collective-permute-done.23
  267.9 11.1 %collective-permute-done.51 = bf16[512,1024]{1,0:T(8,128)(2,1)S(1)} collective-permute-done((bf16[512,1024]{1,0:T(8,128)(2,1)S(1)}, bf16[512,1024]{1,0:T(8,128)(2,1)S(1)}, u32[]{:S(2)}, u32[]{:S(2)}) %collective-permute-start.51) | collective-permute-done | bytes 1048608 | tf_op jit(solution)/shard_map/ppermute | solution.py:64
  285.7 17.9 %collective-permute-done.25 = bf16[512,1024]{1,0:T(8,128)(2,1)S(1)} collective-permute-done((bf16[512,1024]{1,0:T(8,128)(2,1)S(1)}, bf16[512,1024]{1,0:T(8,128)(2,1)S(1)}, u32[]{:S(2)}, u32[]{:S(2)}) %collective-permute-start.25) | collective-permute-done | bytes 1048608 | tf_op jit(solution)/shard_map/ppermute | solution.py:64
  306.9 7.0 fusion.378
  316.0 4.5 fusion.6
  327.0 6.6 fusion.377
  336.1 4.4 fusion.8
  342.0 8.2 multiply_convert_fusion.3
  350.3 8.2 convolution_convert_fusion.3
  362.9 3.7 fusion.12
  366.6 5.4 multiply_convert_fusion.1
  373.4 7.3 fusion.24
  380.8 6.3 convolution_convert_fusion.2
  417.8 7.4 fusion.42
  467.6 13.9 %collective-permute-done.55 = bf16[512,1024]{1,0:T(8,128)(2,1)S(1)} collective-permute-done((bf16[512,1024]{1,0:T(8,128)(2,1)S(1)}, bf16[512,1024]{1,0:T(8,128)(2,1)S(1)}, u32[]{:S(2)}, u32[]{:S(2)}) %collective-permute-start.55) | collective-permute-done | bytes 1048608 | tf_op jit(solution)/shard_map/ppermute | solution.py:64
  483.2 20.8 %collective-permute-done.59 = bf16[512,1024]{1,0:T(8,128)(2,1)S(1)} collective-permute-done((bf16[512,1024]{1,0:T(8,128)(2,1)S(1)}, bf16[512,1024]{1,0:T(8,128)(2,1)S(1)}, u32[]{:S(2)}, u32[]{:S(2)}) %collective-permute-start.59) | collective-permute-done | bytes 1048608 | tf_op jit(solution)/shard_map/ppermute | solution.py:64
  504.5 22.0 %collective-permute-done.63 = bf16[512,1024]{1,0:T(8,128)(2,1)S(1)} collective-permute-done((bf16[512,1024]{1,0:T(8,128)(2,1)S(1)}, bf16[512,1024]{1,0:T(8,128)(2,1)S(1)}, u32[]{:S(2)}, u32[]{:S(2)}) %collective-permute-start.63) | collective-permute-done | bytes 1048608 | tf_op jit(solution)/shard_map/ppermute | solution.py:64
  527.1 21.8 %collective-permute-done.17 = bf16[512,1024]{1,0:T(8,128)(2,1)S(1)} collective-permute-done((bf16[512,1024]{1,0:T(8,128)(2,1)S(1)}, bf16[512,1024]{1,0:T(8,128)(2,1)S(1)}, u32[]{:S(2)}, u32[]{:S(2)}) %collective-permute-start.17) | collective-permute-done | bytes 1048608 | tf_op jit(solution)/shard_map/ppermute | solution.py:64
  549.6 21.8 %collective-permute-done.29 = bf16[512,1024]{1,0:T(8,128)(2,1)S(1)} collective-permute-done((bf16[512,1024]{1,0:T(8,128)(2,1)S(1)}, bf16[512,1024]{1,0:T(8,128)(2,1)S(1)}, u32[]{:S(2)}, u32[]{:S(2)}) %collective-permute-start.29) | collective-permute-done | bytes 1048608 | tf_op jit(solution)/shard_map/ppermute | solution.py:64
  573.8 20.1 %collective-permute-done.33 = bf16[512,1024]{1,0:T(8,128)(2,1)S(1)} collective-permute-done((bf16[512,1024]{1,0:T(8,128)(2,1)S(1)}, bf16[512,1024]{1,0:T(8,128)(2,1)S(1)}, u32[]{:S(2)}, u32[]{:S(2)}) %collective-permute-start.33) | collective-permute-done | bytes 1048608 | tf_op jit(solution)/shard_map/ppermute | solution.py:64
  597.6 18.8 %collective-permute-done.67 = bf16[512,1024]{1,0:T(8,128)(2,1)S(1)} collective-permute-done((bf16[512,1024]{1,0:T(8,128)(2,1)S(1)}, bf16[512,1024]{1,0:T(8,128)(2,1)S(1)}, u32[]{:S(2)}, u32[]{:S(2)}) %collective-permute-start.67) | collective-permute-done | bytes 1048608 | tf_op jit(solution)/shard_map/ppermute | solution.py:64
  620.2 20.7 %collective-permute-start.34 = (bf16[512,1024]{1,0:T(8,128)(2,1)S(1)}, bf16[512,1024]{1,0:T(8,128)(2,1)S(1)}, u32[]{:S(2)}, u32[]{:S(2)}) collective-permute-start(bf16[512,1024]{1,0:T(8,128)(2,1)S(1)} %add_convert_fusion.19), channel_id=1, source_target_pairs={{8,0},{9,1},{10,2},{11,3},{12,4},{13,5},{14,6},{15,7},{0,8},{1,9},... | collective-permute-start | bytes 3145736 | tf_op jit(solution)/shard_map/ppermute | solution.py:64
  641.5 46.5 %collective-permute-done.64 = bf16[512,1024]{1,0:T(8,128)(2,1)S(1)} collective-permute-done((bf16[512,1024]{1,0:T(8,128)(2,1)S(1)}, bf16[512,1024]{1,0:T(8,128)(2,1)S(1)}, u32[]{:S(2)}, u32[]{:S(2)}) %collective-permute-start.64) | collective-permute-done | bytes 1048608 | tf_op jit(solution)/shard_map/ppermute | solution.py:64
  689.4 42.7 %collective-permute-done.34 = bf16[512,1024]{1,0:T(8,128)(2,1)S(1)} collective-permute-done((bf16[512,1024]{1,0:T(8,128)(2,1)S(1)}, bf16[512,1024]{1,0:T(8,128)(2,1)S(1)}, u32[]{:S(2)}, u32[]{:S(2)}) %collective-permute-start.34) | collective-permute-done | bytes 1048608 | tf_op jit(solution)/shard_map/ppermute | solution.py:64
  732.1 3.5 multiply_add_fusion
  742.0 11.1 %fusion = (f32[8,2,512]{2,1,0:T(2,128)S(1)}, f32[8,512,512,2]{2,1,3,0:T(8,128)}) fusion(f32[8,2,512,512]{2,3,1,0:T(8,128)} %get-tuple-element.210, f32[8,2,512]{2,1,0:T(2,128)S(1)} %bitcast.255, bf16[512,8,64,1]{0,2,3,1:T(8,128)(2,1)} %bitcast.246, bf16[512,8,2,64]{0,3,2,1:T(8,128)(2,1)S(1)} %bitcast.240), kind=kOutput, calls=%fused_computation.5 | convolution fusion | flops 549445632 | bytes 35192832 | tf_op jit(solution)/shard_map/while/body/eval_jaxpr/qkgd,skd->kgqs/dot_general | solution.py:388
  753.1 9.2 fusion.52
  764.4 12.4 %fusion.2 = bf16[8,2,512,512]{2,3,1,0:T(8,128)(2,1)S(1)} fusion(f32[8,512,512,2]{2,1,3,0:T(8,128)} %get-tuple-element.220, f32[8,2,512,512]{2,3,1,0:T(8,128)} %get-tuple-element.210, f32[8,2,512]{2,1,0:T(2,128)S(1)} %get-tuple-element.219, f32[8,2,512]{2,1,0:T(2,128)S(1)} %bitcast.257), kind=kLoop, calls=%fused_computation.7 | loop fusion | flops 16777216 | bytes 42008576 | tf_op jit(solution)/shard_map/while/body/eval_jaxpr/convert_element_type | solution.py:392
  797.3 11.3 %collective-permute-done.91 = bf16[512,512]{1,0:T(8,128)(2,1)S(1)} collective-permute-done((bf16[512,512]{1,0:T(8,128)(2,1)S(1)}, bf16[512,512]{1,0:T(8,128)(2,1)S(1)}, u32[]{:S(2)}, u32[]{:S(2)}) %collective-permute-start.91) | collective-permute-done | bytes 524320 | tf_op jit(solution)/shard_map/ppermute | solution.py:68
  809.3 10.7 %collective-permute-done.80 = bf16[512,512]{1,0:T(8,128)(2,1)S(1)} collective-permute-done((bf16[512,512]{1,0:T(8,128)(2,1)S(1)}, bf16[512,512]{1,0:T(8,128)(2,1)S(1)}, u32[]{:S(2)}, u32[]{:S(2)}) %collective-permute-start.80) | collective-permute-done | bytes 524320 | tf_op jit(solution)/shard_map/ppermute | solution.py:68
  820.9 10.0 %collective-permute-done.69 = bf16[512,512]{1,0:T(8,128)(2,1)S(1)} collective-permute-done((bf16[512,512]{1,0:T(8,128)(2,1)S(1)}, bf16[512,512]{1,0:T(8,128)(2,1)S(1)}, u32[]{:S(2)}, u32[]{:S(2)}) %collective-permute-start.69) | collective-permute-done | bytes 524320 | tf_op jit(solution)/shard_map/ppermute | solution.py:68
  874.4 5.0 collective-permute-done.88
  881.2 37.9 %psum.14 = f32[1024]{0:T(1024)S(1)} all-reduce(f32[1024]{0:T(1024)S(1)} %get-tuple-element.53), channel_id=1, replica_groups=mesh['dp'=2,'expert'=16] {'dp','expert'}, use_global_device_ids=true, to_apply=%region_47.48 | all-reduce | flops 1024 | bytes 8192 | tf_op jit(solution)/shard_map/psum | solution.py:452
  (640 shorter events, 275.1 us)
Async XLA Ops:
  7.2 131.9 %collective-permute-start.38 = (bf16[512,1024]{1,0:T(8,128)(2,1)}, bf16[512,1024]{1,0:T(8,128)(2,1)}, u32[]{:S(2)}, u32[]{:S(2)}) collective-permute-start(bf16[512,1024]{1,0:T(8,128)(2,1)} %param.25), channel_id=1, source_target_pairs={{1,0},{0,1},{3,2},{2,3},{5,4},{4,5},{7,6},{6,7},{9,8},{8,9},{11,10... | collective-permute-start | bytes 3145736 | tf_op jit(solution)/shard_map/ppermute | solution.py:64
  7.7 133.4 %collective-permute-start.39 = (bf16[512,1024]{1,0:T(8,128)(2,1)}, bf16[512,1024]{1,0:T(8,128)(2,1)}, u32[]{:S(2)}, u32[]{:S(2)}) collective-permute-start(bf16[512,1024]{1,0:T(8,128)(2,1)} %param.25), channel_id=1, source_target_pairs={{2,0},{3,1},{0,2},{1,3},{6,4},{7,5},{4,6},{5,7},{10,8},{11,9},{8,1... | collective-permute-start | bytes 3145736 | tf_op jit(solution)/shard_map/ppermute | solution.py:64
  10.3 135.4 %collective-permute-start.41 = (bf16[512,1024]{1,0:T(8,128)(2,1)}, bf16[512,1024]{1,0:T(8,128)(2,1)}, u32[]{:S(2)}, u32[]{:S(2)}) collective-permute-start(bf16[512,1024]{1,0:T(8,128)(2,1)} %param.25), channel_id=1, source_target_pairs={{4,0},{5,1},{6,2},{7,3},{8,4},{9,5},{10,6},{11,7},{12,8},{13,9},{1... | collective-permute-start | bytes 3145736 | tf_op jit(solution)/shard_map/ppermute | solution.py:64
  15.0 29.5 %collective-permute-start.2 = (bf16[256,1024]{1,0:T(8,128)(2,1)S(1)}, bf16[256,1024]{1,0:T(8,128)(2,1)S(1)}, u32[]{:S(2)}, u32[]{:S(2)}) collective-permute-start(bf16[256,1024]{1,0:T(8,128)(2,1)S(1)} %constant_dynamic-slice_fusion.23), channel_id=1, source_target_pairs={{0,16},{16,0},{1,17},{17,1},{2,18},{18,2},{3,19},{19,3},{4,20},{20... | collective-permute-start | bytes 1572872 | tf_op jit(solution)/shard_map/ppermute | solution.py:68
  17.7 25.9 %collective-permute-start = (bf16[256,1024]{1,0:T(8,128)(2,1)S(1)}, bf16[256,1024]{1,0:T(8,128)(2,1)S(1)}, u32[]{:S(2)}, u32[]{:S(2)}) collective-permute-start(bf16[256,1024]{1,0:T(8,128)(2,1)S(1)} %constant_dynamic-slice_fusion.24), channel_id=1, source_target_pairs={{0,16},{16,0},{1,17},{17,1},{2,18},{18,2},{3,19},{19,3},{4,20},{20... | collective-permute-start | bytes 1572872 | tf_op jit(solution)/shard_map/ppermute | solution.py:68
  59.2 84.4 %collective-permute-start.45 = (bf16[512,1024]{1,0:T(8,128)(2,1)}, bf16[512,1024]{1,0:T(8,128)(2,1)}, u32[]{:S(2)}, u32[]{:S(2)}) collective-permute-start(bf16[512,1024]{1,0:T(8,128)(2,1)} %param.25), channel_id=1, source_target_pairs={{12,0},{13,1},{14,2},{15,3},{0,4},{1,5},{2,6},{3,7},{4,8},{5,9},{6... | collective-permute-start | bytes 3145736 | tf_op jit(solution)/shard_map/ppermute | solution.py:64
  59.2 35.2 %collective-permute-start.5 = (bf16[256,1024]{1,0:T(8,128)(2,1)}, bf16[256,1024]{1,0:T(8,128)(2,1)}, u32[]{:S(2)}, u32[]{:S(2)}) collective-permute-start(bf16[256,1024]{1,0:T(8,128)(2,1)} %collective-permute-done.4), channel_id=1, source_target_pairs={{1,0},{0,1},{3,2},{2,3},{5,4},{4,5},{7,6},{6,7},{9,8},{8,9},{11,10... | collective-permute-start | bytes 1572872 | tf_op jit(solution)/shard_map/ppermute | solution.py:64
  106.6 40.7 %collective-permute-start.19 = (bf16[512,1024]{1,0:T(8,128)(2,1)S(1)}, bf16[512,1024]{1,0:T(8,128)(2,1)S(1)}, u32[]{:S(2)}, u32[]{:S(2)}) collective-permute-start(bf16[512,1024]{1,0:T(8,128)(2,1)S(1)} %multiply_convert_fusion.6), channel_id=1, source_target_pairs={{12,0},{13,1},{14,2},{15,3},{0,4},{1,5},{2,6},{3,7},{4,8},{5,9},{6... | collective-permute-start | bytes 3145736 | tf_op jit(solution)/shard_map/ppermute | solution.py:64
  141.1 26.1 %collective-permute-start.7 = (bf16[512,1024]{1,0:T(8,128)(2,1)S(1)}, bf16[512,1024]{1,0:T(8,128)(2,1)S(1)}, u32[]{:S(2)}, u32[]{:S(2)}) collective-permute-start(bf16[512,1024]{1,0:T(8,128)(2,1)S(1)} %multiply_convert_fusion.6), channel_id=1, source_target_pairs={{2,0},{3,1},{0,2},{1,3},{6,4},{7,5},{4,6},{5,7},{10,8},{11,9},{8,1... | collective-permute-start | bytes 3145736 | tf_op jit(solution)/shard_map/ppermute | solution.py:64
  145.7 26.1 %collective-permute-start.9 = (bf16[512,1024]{1,0:T(8,128)(2,1)S(1)}, bf16[512,1024]{1,0:T(8,128)(2,1)S(1)}, u32[]{:S(2)}, u32[]{:S(2)}) collective-permute-start(bf16[512,1024]{1,0:T(8,128)(2,1)S(1)} %multiply_convert_fusion.6), channel_id=1, source_target_pairs={{4,0},{5,1},{6,2},{7,3},{8,4},{9,5},{10,6},{11,7},{12,8},{13,9},{1... | collective-permute-start | bytes 3145736 | tf_op jit(solution)/shard_map/ppermute | solution.py:64
  148.8 40.9 %collective-permute-start.43 = (bf16[512,1024]{1,0:T(8,128)(2,1)}, bf16[512,1024]{1,0:T(8,128)(2,1)S(1)}, u32[]{:S(2)}, u32[]{:S(2)}) collective-permute-start(bf16[512,1024]{1,0:T(8,128)(2,1)} %collective-permute-done.41), channel_id=1, source_target_pairs={{2,0},{3,1},{0,2},{1,3},{6,4},{7,5},{4,6},{5,7},{10,8},{11,9},{8,1... | collective-permute-start | bytes 3145736 | tf_op jit(solution)/shard_map/ppermute | solution.py:64
  167.7 44.4 %collective-permute-start.47 = (bf16[512,1024]{1,0:T(8,128)(2,1)}, bf16[512,1024]{1,0:T(8,128)(2,1)S(1)}, u32[]{:S(2)}, u32[]{:S(2)}) collective-permute-start(bf16[512,1024]{1,0:T(8,128)(2,1)} %collective-permute-done.45), channel_id=1, source_target_pairs={{2,0},{3,1},{0,2},{1,3},{6,4},{7,5},{4,6},{5,7},{10,8},{11,9},{8,1... | collective-permute-start | bytes 3145736 | tf_op jit(solution)/shard_map/ppermute | solution.py:64
  170.8 42.0 %collective-permute-start.8 = (bf16[512,1024]{1,0:T(8,128)(2,1)S(1)}, bf16[512,1024]{1,0:T(8,128)(2,1)S(1)}, u32[]{:S(2)}, u32[]{:S(2)}) collective-permute-start(bf16[512,1024]{1,0:T(8,128)(2,1)S(1)} %collective-permute-done.7), channel_id=1, source_target_pairs={{1,0},{0,1},{3,2},{2,3},{5,4},{4,5},{7,6},{6,7},{9,8},{8,9},{11,10... | collective-permute-start | bytes 3145736 | tf_op jit(solution)/shard_map/ppermute | solution.py:64
  171.8 49.0 %collective-permute-start.49 = (bf16[512,1024]{1,0:T(8,128)(2,1)}, bf16[512,1024]{1,0:T(8,128)(2,1)S(1)}, u32[]{:S(2)}, u32[]{:S(2)}) collective-permute-start(bf16[512,1024]{1,0:T(8,128)(2,1)} %param.25), channel_id=1, source_target_pairs={{8,0},{9,1},{10,2},{11,3},{12,4},{13,5},{14,6},{15,7},{0,8},{1,9},... | collective-permute-start | bytes 3145736 | tf_op jit(solution)/shard_map/ppermute | solution.py:64
  189.7 31.1 %collective-permute-start.10 = (bf16[512,1024]{1,0:T(8,128)(2,1)S(1)}, bf16[512,1024]{1,0:T(8,128)(2,1)S(1)}, u32[]{:S(2)}, u32[]{:S(2)}) collective-permute-start(bf16[512,1024]{1,0:T(8,128)(2,1)S(1)} %collective-permute-done.9), channel_id=1, source_target_pairs={{1,0},{0,1},{3,2},{2,3},{5,4},{4,5},{7,6},{6,7},{9,8},{8,9},{11,10... | collective-permute-start | bytes 3145736 | tf_op jit(solution)/shard_map/ppermute | solution.py:64
  190.3 44.3 %collective-permute-start.11 = (bf16[512,1024]{1,0:T(8,128)(2,1)S(1)}, bf16[512,1024]{1,0:T(8,128)(2,1)S(1)}, u32[]{:S(2)}, u32[]{:S(2)}) collective-permute-start(bf16[512,1024]{1,0:T(8,128)(2,1)S(1)} %collective-permute-done.9), channel_id=1, source_target_pairs={{2,0},{3,1},{0,2},{1,3},{6,4},{7,5},{4,6},{5,7},{10,8},{11,9},{8,1... | collective-permute-start | bytes 3145736 | tf_op jit(solution)/shard_map/ppermute | solution.py:64
  212.8 44.3 %collective-permute-start.21 = (bf16[512,1024]{1,0:T(8,128)(2,1)S(1)}, bf16[512,1024]{1,0:T(8,128)(2,1)S(1)}, u32[]{:S(2)}, u32[]{:S(2)}) collective-permute-start(bf16[512,1024]{1,0:T(8,128)(2,1)S(1)} %collective-permute-done.19), channel_id=1, source_target_pairs={{2,0},{3,1},{0,2},{1,3},{6,4},{7,5},{4,6},{5,7},{10,8},{11,9},{8,1... | collective-permute-start | bytes 3145736 | tf_op jit(solution)/shard_map/ppermute | solution.py:64
  220.7 47.2 %collective-permute-start.23 = (bf16[512,1024]{1,0:T(8,128)(2,1)S(1)}, bf16[512,1024]{1,0:T(8,128)(2,1)S(1)}, u32[]{:S(2)}, u32[]{:S(2)}) collective-permute-start(bf16[512,1024]{1,0:T(8,128)(2,1)S(1)} %multiply_convert_fusion.6), channel_id=1, source_target_pairs={{8,0},{9,1},{10,2},{11,3},{12,4},{13,5},{14,6},{15,7},{0,8},{1,9},... | collective-permute-start | bytes 3145736 | tf_op jit(solution)/shard_map/ppermute | solution.py:64
  220.8 58.3 %collective-permute-start.51 = (bf16[512,1024]{1,0:T(8,128)(2,1)S(1)}, bf16[512,1024]{1,0:T(8,128)(2,1)S(1)}, u32[]{:S(2)}, u32[]{:S(2)}) collective-permute-start(bf16[512,1024]{1,0:T(8,128)(2,1)S(1)} %collective-permute-done.49), channel_id=1, source_target_pairs={{2,0},{3,1},{0,2},{1,3},{6,4},{7,5},{4,6},{5,7},{10,8},{11,9},{8,1... | collective-permute-start | bytes 3145736 | tf_op jit(solution)/shard_map/ppermute | solution.py:64
  234.6 45.0 %collective-permute-start.48 = (bf16[512,1024]{1,0:T(8,128)(2,1)S(1)}, bf16[512,1024]{1,0:T(8,128)(2,1)S(1)}, u32[]{:S(2)}, u32[]{:S(2)}) collective-permute-start(bf16[512,1024]{1,0:T(8,128)(2,1)S(1)} %collective-permute-done.47), channel_id=1, source_target_pairs={{1,0},{0,1},{3,2},{2,3},{5,4},{4,5},{7,6},{6,7},{9,8},{8,9},{11,10... | collective-permute-start | bytes 3145736 | tf_op jit(solution)/shard_map/ppermute | solution.py:64
  235.6 45.2 %collective-permute-start.50 = (bf16[512,1024]{1,0:T(8,128)(2,1)S(1)}, bf16[512,1024]{1,0:T(8,128)(2,1)S(1)}, u32[]{:S(2)}, u32[]{:S(2)}) collective-permute-start(bf16[512,1024]{1,0:T(8,128)(2,1)S(1)} %collective-permute-done.49), channel_id=1, source_target_pairs={{1,0},{0,1},{3,2},{2,3},{5,4},{4,5},{7,6},{6,7},{9,8},{8,9},{11,10... | collective-permute-start | bytes 3145736 | tf_op jit(solution)/shard_map/ppermute | solution.py:64
  257.1 49.8 %collective-permute-start.13 = (bf16[512,1024]{1,0:T(8,128)(2,1)S(1)}, bf16[512,1024]{1,0:T(8,128)(2,1)S(1)}, u32[]{:S(2)}, u32[]{:S(2)}) collective-permute-start(bf16[512,1024]{1,0:T(8,128)(2,1)S(1)} %bitcast.390), channel_id=1, source_target_pairs={{0,16},{16,0},{1,17},{17,1},{2,18},{18,2},{3,19},{19,3},{4,20},{20... | collective-permute-start | bytes 3145736 | tf_op jit(solution)/shard_map/ppermute | solution.py:68
  279.0 24.6 %collective-permute-start.25 = (bf16[512,1024]{1,0:T(8,128)(2,1)S(1)}, bf16[512,1024]{1,0:T(8,128)(2,1)S(1)}, u32[]{:S(2)}, u32[]{:S(2)}) collective-permute-start(bf16[512,1024]{1,0:T(8,128)(2,1)S(1)} %collective-permute-done.23), channel_id=1, source_target_pairs={{2,0},{3,1},{0,2},{1,3},{6,4},{7,5},{4,6},{5,7},{10,8},{11,9},{8,1... | collective-permute-start | bytes 3145736 | tf_op jit(solution)/shard_map/ppermute | solution.py:64
  282.7 32.4 %collective-permute-start.14 = (bf16[512,512]{1,0:T(8,128)(2,1)S(1)}, bf16[512,512]{1,0:T(8,128)(2,1)S(1)}, u32[]{:S(2)}, u32[]{:S(2)}) collective-permute-start(bf16[512,512]{1,0:T(8,128)(2,1)S(1)} %bitcast.394), channel_id=1, source_target_pairs={{0,16},{16,0},{1,17},{17,1},{2,18},{18,2},{3,19},{19,3},{4,20},{20... | collective-permute-start | bytes 1572872 | tf_op jit(solution)/shard_map/ppermute | solution.py:68
  285.0 38.1 %collective-permute-start.24 = (bf16[512,1024]{1,0:T(8,128)(2,1)S(1)}, bf16[512,1024]{1,0:T(8,128)(2,1)S(1)}, u32[]{:S(2)}, u32[]{:S(2)}) collective-permute-start(bf16[512,1024]{1,0:T(8,128)(2,1)S(1)} %collective-permute-done.23), channel_id=1, source_target_pairs={{1,0},{0,1},{3,2},{2,3},{5,4},{4,5},{7,6},{6,7},{9,8},{8,9},{11,10... | collective-permute-start | bytes 3145736 | tf_op jit(solution)/shard_map/ppermute | solution.py:64
  430.3 490.7 %all-reduce.2.cloned.1.call-start = ((), (), s32[]{:S(2)}) async-start(), calls=%async_computation.3 | async-start | bytes 196608 | tf_op jit(solution)/shard_map/psum | solution.py:448
  433.8 25.6 %collective-permute-start.101 = (bf16[512,1024]{1,0:T(8,128)(2,1)}, bf16[512,1024]{1,0:T(8,128)(2,1)}, u32[]{:S(2)}, u32[]{:S(2)}) collective-permute-start(bf16[512,1024]{1,0:T(8,128)(2,1)} %dynamic-slice_convert_fusion), channel_id=1, source_target_pairs={{0,16},{16,0},{1,17},{17,1},{2,18},{18,2},{3,19},{19,3},{4,20},{20... | collective-permute-start | bytes 3145736 | tf_op jit(solution)/shard_map/ppermute | solution.py:68
  455.6 26.0 %collective-permute-start.55 = (bf16[512,1024]{1,0:T(8,128)(2,1)S(1)}, bf16[512,1024]{1,0:T(8,128)(2,1)S(1)}, u32[]{:S(2)}, u32[]{:S(2)}) collective-permute-start(bf16[512,1024]{1,0:T(8,128)(2,1)S(1)} %add_convert_fusion.13), channel_id=1, source_target_pairs={{2,0},{3,1},{0,2},{1,3},{6,4},{7,5},{4,6},{5,7},{10,8},{11,9},{8,1... | collective-permute-start | bytes 3145736 | tf_op jit(solution)/shard_map/ppermute | solution.py:64
  459.4 44.6 %collective-permute-start.59 = (bf16[512,1024]{1,0:T(8,128)(2,1)S(1)}, bf16[512,1024]{1,0:T(8,128)(2,1)S(1)}, u32[]{:S(2)}, u32[]{:S(2)}) collective-permute-start(bf16[512,1024]{1,0:T(8,128)(2,1)S(1)} %add_convert_fusion.10), channel_id=1, source_target_pairs={{2,0},{3,1},{0,2},{1,3},{6,4},{7,5},{4,6},{5,7},{10,8},{11,9},{8,1... | collective-permute-start | bytes 3145736 | tf_op jit(solution)/shard_map/ppermute | solution.py:64
  464.1 62.4 %collective-permute-start.63 = (bf16[512,1024]{1,0:T(8,128)(2,1)S(1)}, bf16[512,1024]{1,0:T(8,128)(2,1)S(1)}, u32[]{:S(2)}, u32[]{:S(2)}) collective-permute-start(bf16[512,1024]{1,0:T(8,128)(2,1)S(1)} %add_convert_fusion.7), channel_id=1, source_target_pairs={{2,0},{3,1},{0,2},{1,3},{6,4},{7,5},{4,6},{5,7},{10,8},{11,9},{8,1... | collective-permute-start | bytes 3145736 | tf_op jit(solution)/shard_map/ppermute | solution.py:64
  464.9 84.1 %collective-permute-start.17 = (bf16[512,1024]{1,0:T(8,128)(2,1)S(1)}, bf16[512,1024]{1,0:T(8,128)(2,1)S(1)}, u32[]{:S(2)}, u32[]{:S(2)}) collective-permute-start(bf16[512,1024]{1,0:T(8,128)(2,1)S(1)} %add_convert_fusion.26), channel_id=1, source_target_pairs={{2,0},{3,1},{0,2},{1,3},{6,4},{7,5},{4,6},{5,7},{10,8},{11,9},{8,1... | collective-permute-start | bytes 3145736 | tf_op jit(solution)/shard_map/ppermute | solution.py:64
  466.8 104.7 %collective-permute-start.29 = (bf16[512,1024]{1,0:T(8,128)(2,1)S(1)}, bf16[512,1024]{1,0:T(8,128)(2,1)S(1)}, u32[]{:S(2)}, u32[]{:S(2)}) collective-permute-start(bf16[512,1024]{1,0:T(8,128)(2,1)S(1)} %add_convert_fusion.23), channel_id=1, source_target_pairs={{2,0},{3,1},{0,2},{1,3},{6,4},{7,5},{4,6},{5,7},{10,8},{11,9},{8,1... | collective-permute-start | bytes 3145736 | tf_op jit(solution)/shard_map/ppermute | solution.py:64
  481.6 112.4 %collective-permute-start.33 = (bf16[512,1024]{1,0:T(8,128)(2,1)S(1)}, bf16[512,1024]{1,0:T(8,128)(2,1)S(1)}, u32[]{:S(2)}, u32[]{:S(2)}) collective-permute-start(bf16[512,1024]{1,0:T(8,128)(2,1)S(1)} %add_convert_fusion.20), channel_id=1, source_target_pairs={{2,0},{3,1},{0,2},{1,3},{6,4},{7,5},{4,6},{5,7},{10,8},{11,9},{8,1... | collective-permute-start | bytes 3145736 | tf_op jit(solution)/shard_map/ppermute | solution.py:64
  504.0 92.0 %collective-permute-start.35 = (bf16[512,1024]{1,0:T(8,128)(2,1)S(1)}, bf16[512,1024]{1,0:T(8,128)(2,1)S(1)}, u32[]{:S(2)}, u32[]{:S(2)}) collective-permute-start(bf16[512,1024]{1,0:T(8,128)(2,1)S(1)} %copy-done.37), channel_id=1, source_target_pairs={{1,0},{0,1},{3,2},{2,3},{5,4},{4,5},{7,6},{6,7},{9,8},{8,9},{11,10... | collective-permute-start | bytes 3145736 | tf_op jit(solution)/shard_map/ppermute | solution.py:64
  526.5 89.9 %collective-permute-start.67 = (bf16[512,1024]{1,0:T(8,128)(2,1)S(1)}, bf16[512,1024]{1,0:T(8,128)(2,1)S(1)}, u32[]{:S(2)}, u32[]{:S(2)}) collective-permute-start(bf16[512,1024]{1,0:T(8,128)(2,1)S(1)} %add_convert_fusion.4), channel_id=1, source_target_pairs={{2,0},{3,1},{0,2},{1,3},{6,4},{7,5},{4,6},{5,7},{10,8},{11,9},{8,1... | collective-permute-start | bytes 3145736 | tf_op jit(solution)/shard_map/ppermute | solution.py:64
  549.0 68.1 %collective-permute-start.56 = (bf16[512,1024]{1,0:T(8,128)(2,1)S(1)}, bf16[512,1024]{1,0:T(8,128)(2,1)S(1)}, u32[]{:S(2)}, u32[]{:S(2)}) collective-permute-start(bf16[512,1024]{1,0:T(8,128)(2,1)S(1)} %add_convert_fusion.12), channel_id=1, source_target_pairs={{12,0},{13,1},{14,2},{15,3},{0,4},{1,5},{2,6},{3,7},{4,8},{5,9},{6... | collective-permute-start | bytes 3145736 | tf_op jit(solution)/shard_map/ppermute | solution.py:64
  571.4 48.8 %collective-permute-start.60 = (bf16[512,1024]{1,0:T(8,128)(2,1)S(1)}, bf16[512,1024]{1,0:T(8,128)(2,1)S(1)}, u32[]{:S(2)}, u32[]{:S(2)}) collective-permute-start(bf16[512,1024]{1,0:T(8,128)(2,1)S(1)} %add_convert_fusion.9), channel_id=1, source_target_pairs={{4,0},{5,1},{6,2},{7,3},{8,4},{9,5},{10,6},{11,7},{12,8},{13,9},{1... | collective-permute-start | bytes 3145736 | tf_op jit(solution)/shard_map/ppermute | solution.py:64
  593.9 94.1 %collective-permute-start.64 = (bf16[512,1024]{1,0:T(8,128)(2,1)S(1)}, bf16[512,1024]{1,0:T(8,128)(2,1)S(1)}, u32[]{:S(2)}, u32[]{:S(2)}) collective-permute-start(bf16[512,1024]{1,0:T(8,128)(2,1)S(1)} %add_convert_fusion.6), channel_id=1, source_target_pairs={{8,0},{9,1},{10,2},{11,3},{12,4},{13,5},{14,6},{15,7},{0,8},{1,9},... | collective-permute-start | bytes 3145736 | tf_op jit(solution)/shard_map/ppermute | solution.py:64
  596.1 93.3 %collective-permute-start.37 = (bf16[512,1024]{1,0:T(8,128)(2,1)S(1)}, bf16[512,1024]{1,0:T(8,128)(2,1)S(1)}, u32[]{:S(2)}, u32[]{:S(2)}) collective-permute-start(bf16[512,1024]{1,0:T(8,128)(2,1)S(1)} %add_convert_fusion.17), channel_id=1, source_target_pairs={{2,0},{3,1},{0,2},{1,3},{6,4},{7,5},{4,6},{5,7},{10,8},{11,9},{8,1... | collective-permute-start | bytes 3145736 | tf_op jit(solution)/shard_map/ppermute | solution.py:64
  616.4 73.0 %collective-permute-start.18 = (bf16[512,1024]{1,0:T(8,128)(2,1)S(1)}, bf16[512,1024]{1,0:T(8,128)(2,1)S(1)}, u32[]{:S(2)}, u32[]{:S(2)}) collective-permute-start(bf16[512,1024]{1,0:T(8,128)(2,1)S(1)} %add_convert_fusion.25), channel_id=1, source_target_pairs={{12,0},{13,1},{14,2},{15,3},{0,4},{1,5},{2,6},{3,7},{4,8},{5,9},{6... | collective-permute-start | bytes 3145736 | tf_op jit(solution)/shard_map/ppermute | solution.py:64
  617.1 72.4 %collective-permute-start.30 = (bf16[512,1024]{1,0:T(8,128)(2,1)S(1)}, bf16[512,1024]{1,0:T(8,128)(2,1)S(1)}, u32[]{:S(2)}, u32[]{:S(2)}) collective-permute-start(bf16[512,1024]{1,0:T(8,128)(2,1)S(1)} %add_convert_fusion.22), channel_id=1, source_target_pairs={{4,0},{5,1},{6,2},{7,3},{8,4},{9,5},{10,6},{11,7},{12,8},{13,9},{1... | collective-permute-start | bytes 3145736 | tf_op jit(solution)/shard_map/ppermute | solution.py:64
  620.2 111.9 %collective-permute-start.34 = (bf16[512,1024]{1,0:T(8,128)(2,1)S(1)}, bf16[512,1024]{1,0:T(8,128)(2,1)S(1)}, u32[]{:S(2)}, u32[]{:S(2)}) collective-permute-start(bf16[512,1024]{1,0:T(8,128)(2,1)S(1)} %add_convert_fusion.19), channel_id=1, source_target_pairs={{8,0},{9,1},{10,2},{11,3},{12,4},{13,5},{14,6},{15,7},{0,8},{1,9},... | collective-permute-start | bytes 3145736 | tf_op jit(solution)/shard_map/ppermute | solution.py:64
  764.4 28.8 %collective-permute-start.90 = (bf16[1024,512]{1,0:T(8,128)(2,1)S(1)}, bf16[1024,512]{1,0:T(8,128)(2,1)S(1)}, u32[]{:S(2)}, u32[]{:S(2)}) collective-permute-start(bf16[1024,512]{1,0:T(8,128)(2,1)S(1)} %constant_dynamic-slice_fusion.7), channel_id=1, source_target_pairs={{1,0},{0,1},{3,2},{2,3},{5,4},{4,5},{7,6},{6,7},{9,8},{8,9},{11,10... | collective-permute-start | bytes 3145736 | tf_op jit(solution)/shard_map/ppermute | solution.py:64
  794.7 25.3 %collective-permute-start.80 = (bf16[512,512]{1,0:T(8,128)(2,1)S(1)}, bf16[512,512]{1,0:T(8,128)(2,1)S(1)}, u32[]{:S(2)}, u32[]{:S(2)}) collective-permute-start(bf16[512,512]{1,0:T(8,128)(2,1)S(1)} %constant_dynamic-slice_fusion.13), channel_id=1, source_target_pairs={{0,16},{16,0},{1,17},{17,1},{2,18},{18,2},{3,19},{19,3},{4,20},{20... | collective-permute-start | bytes 1572872 | tf_op jit(solution)/shard_map/ppermute | solution.py:68
  796.7 34.2 %collective-permute-start.69 = (bf16[512,512]{1,0:T(8,128)(2,1)S(1)}, bf16[512,512]{1,0:T(8,128)(2,1)S(1)}, u32[]{:S(2)}, u32[]{:S(2)}) collective-permute-start(bf16[512,512]{1,0:T(8,128)(2,1)S(1)} %constant_dynamic-slice_fusion.20), channel_id=1, source_target_pairs={{0,16},{16,0},{1,17},{17,1},{2,18},{18,2},{3,19},{19,3},{4,20},{20... | collective-permute-start | bytes 1572872 | tf_op jit(solution)/shard_map/ppermute | solution.py:68
  869.4 50.3 %collective-permute-start.77 = (bf16[256,512]{1,0:T(8,128)(2,1)S(1)}, bf16[256,512]{1,0:T(8,128)(2,1)}, u32[]{:S(2)}, u32[]{:S(2)}) collective-permute-start(bf16[256,512]{1,0:T(8,128)(2,1)S(1)} %constant_dynamic-slice_fusion.15), channel_id=1, source_target_pairs={{2,0},{3,1},{0,2},{1,3},{6,4},{7,5},{4,6},{5,7},{10,8},{11,9},{8,1... | collective-permute-start | bytes 786440 | tf_op jit(solution)/shard_map/ppermute | solution.py:64
  874.3 49.5 %collective-permute-start.100 = (bf16[512,512]{1,0:T(8,128)(2,1)S(1)}, bf16[512,512]{1,0:T(8,128)(2,1)}, u32[]{:S(2)}, u32[]{:S(2)}) collective-permute-start(bf16[512,512]{1,0:T(8,128)(2,1)S(1)} %maximum_select_fusion.13), channel_id=1, source_target_pairs={{1,0},{0,1},{3,2},{2,3},{5,4},{4,5},{7,6},{6,7},{9,8},{8,9},{11,10... | collective-permute-start | bytes 1572872 | tf_op jit(solution)/shard_map/ppermute | solution.py:64
  879.6 47.1 %collective-permute-start.89 = (bf16[512,512]{1,0:T(8,128)(2,1)S(1)}, bf16[512,512]{1,0:T(8,128)(2,1)}, u32[]{:S(2)}, u32[]{:S(2)}) collective-permute-start(bf16[512,512]{1,0:T(8,128)(2,1)S(1)} %maximum_select_fusion.12), channel_id=1, source_target_pairs={{1,0},{0,1},{3,2},{2,3},{5,4},{4,5},{7,6},{6,7},{9,8},{8,9},{11,10... | collective-permute-start | bytes 1572872 | tf_op jit(solution)/shard_map/ppermute | solution.py:64
  (170 other events, 1803.8 us)
Sparse Core Ops, SparseCore 0:
  763.2 121.3 all-reduce.1

commit v2 on v1

--- a/solution.py
+++ b/solution.py
@@ -236,7 +236,10 @@
         )
         for n, offset in enumerate(offsets)
     }
-    cot_rows = gather_rows(cotangent, owners)
+    cot_all = lax.all_gather(cotangent, "expert", axis=0, tiled=True)
+    cot_rows = {
+        offset: piece(cot_all, sources[n], sequence_length) for n, offset in enumerate(offsets)
+    }
     full_in = whole_expert(expert_in[0])
     full_down = whole_expert(expert_down[0])
     resid_in = hidden.astype(single_float)
@@ -299,7 +302,7 @@
         for part in (near_first[:split], near_first[split:])
         if part
     ]
-    out_parts, grad_parts, gate_parts = ({}, {}, {})
+    scaled_parts, grad_parts, gate_parts = ({}, {}, {})
     in_part, down_part = (0.0, 0.0)
     for group in groups:
         pick = lambda rows: jnp.concatenate(
@@ -351,9 +354,7 @@
             grad_parts[o] = jnp.einsum(
                 "ct,cd->td", low, row_grads[span], preferred_element_type=single_float
             ).astype(brain_float_half)
-            out_parts[o] = jnp.einsum(
-                "ct,cd->td", low, scaled_out[span], preferred_element_type=single_float
-            ).astype(brain_float_half)
+            scaled_parts[o] = scaled_out[span]
             gate_parts[o] = jnp.sum(jnp.where(select[o], slot_grad[span][:, None], 0.0), axis=0)
     returned_gates = jnp.zeros((owners, sequence_length), single_float).at[sources].set(
         jnp.stack([gate_parts[o] for o in offsets]), unique_indices=True
@@ -365,7 +366,19 @@
     router_part = jnp.einsum("sd,se->ed", moe_in, logit_grad, preferred_element_type=single_float)
     moe_grad = jnp.einsum("se,de->sd", logit_grad, full_router, preferred_element_type=single_float)
     moe_grad = moe_grad + scatter_rows(grad_parts, owners)
-    block_out = (first_sum + scatter_rows(out_parts, owners)).astype(brain_float_half)
+    places = jnp.zeros((owners,), jnp.int32).at[sources].set(
+        jnp.arange(owners, dtype=jnp.int32), unique_indices=True
+    )
+    places, moe_grad = lax.optimization_barrier((places, moe_grad))
+    scaled_all = jnp.stack([scaled_parts[o] for o in offsets])[places]
+    select_all = (
+        jnp.arange(capacity, dtype=jnp.int32)[None, :, None].astype(single_float)
+        == slots_here[places][:, None, :]
+    ).astype(brain_float_half)
+    mixture = jnp.einsum(
+        "nct,ncd->ntd", select_all, scaled_all, preferred_element_type=single_float
+    ).astype(brain_float_half)
+    mixture = lax.psum_scatter(mixture, "expert", scatter_dimension=0, tiled=True)[0]
     expert_in_share = fold_expert(in_part)[None]
     expert_down_share = fold_expert(down_part)[None]
     ffn_gain_part = jnp.sum(moe_grad * normal_two, axis=0)
@@ -443,19 +456,30 @@
     hidden_grad = (
         first_grad + norm_backward(normed_grad, gain_attn, normal_one, inverse_one)
     ).astype(brain_float_half)
+    mixture, hidden_grad = lax.optimization_barrier((mixture, hidden_grad))
+    block_out = (first_sum + mixture.astype(single_float)).astype(brain_float_half)
     side = lax.axis_index("dp")
     own = model_width // lax.axis_size("dp")
-    early = lax.psum(
-        jnp.concatenate([ffn_gain_part[None], router_part], axis=0), ("dp", "expert")
-    )
-    early = lax.dynamic_slice_in_dim(early, side * own, own, 1)
-    late = lax.dynamic_slice_in_dim(lax.psum(attn_gain_part, ("dp", "expert")), side * own, own, 0)
+
+    def total_small(rows):
+        if lax.axis_size("dp") != 2:
+            return lax.dynamic_slice_in_dim(lax.psum(rows, ("dp", "expert")), side * own, own, 1)
+        rows = piece(rows, side, own, 1) + swap_dp(piece(rows, 1 - side, own, 1))
+        copies = jnp.broadcast_to(rows[None], (owners,) + rows.shape)
+        return jnp.sum(
+            lax.all_to_all(copies, "expert", split_axis=0, concat_axis=0, tiled=True), axis=0
+        )
+
+    early = total_small(jnp.concatenate([ffn_gain_part[None], router_part], axis=0))
+    late = total_small(attn_gain_part[None])[0]
+    query_keyval = fold_shared(jnp.concatenate([query_part, keyval_part], axis=1), owners)
+    query_share, keyval_share = (query_keyval[:, :model_width], query_keyval[:, model_width:])
     return (
         block_out,
         hidden_grad,
         late,
-        fold_shared(query_part, owners),
-        fold_shared(keyval_part, owners),
+        query_share,
+        keyval_share,
         fold_shared(out_part, owners),
         early[0],
         early[1:].T,

time: 946 us -> 884 us (0.934)
  waiting for transfers between devices: 446 us -> 330 us
  local copies, waits for them, and re-layouts: 33.9 us -> 87.4 us
  blocking collectives: 60 us -> 29.1 us
  other arithmetic: 67.4 us -> 84.4 us
  matrix products: 198 us -> 210 us
    ppermute x93 -> x53, waiting for transfers between devices: 377 us -> 246 us  [at_offset(): return lax.ppermute(arr, 'expert', pairs)]
    unnamed x256 -> x271, local copies, waits for them, and re-layouts: 10.5 us -> 50.5 us
    ppermute x93 -> x53, starting transfers between devices: 91.6 us -> 53.7 us  [at_offset(): return lax.ppermute(arr, 'expert', pairs)]
    psum x1 -> x0, blocking collectives: 37.9 us -> none  [on_device(): lax.psum(attn_gain_part, ('dp', 'expert'))]
    all_to_all x2, waiting for transfers between devices: 22.5 us -> 44 us  [to_owners(): lax.all_to_all(columns.T, 'expert', split_axis=0, concat_axis=0, tiled=True)]
    all_to_all x1, starting transfers between devices: 3.5 us -> 24.7 us  [on_device(): lax.all_to_all(returned_gates, 'expert', split_axis=0, concat_axis=0, til...]
    all_to_all x0 -> x2, starting transfers between devices: none -> 12.3 us  [total_small(): lax.all_to_all(copies, 'expert', split_axis=0, concat_axis=0, tiled=True)]
    dot_general x32, matrix products: 30.3 us -> 40.1 us  [on_device(): jnp.dot(select[o].astype(brain_float_half), rows[o], preferred_element_ty...]
  transfers between devices with their start and end apart: 107 -> 71, of which waited for: 37 -> 24; matrix products, arithmetic and copies ran while one was open for 18% -> 29% of each run, Pallas kernels for 0% -> 0%
where the time goes in v2:
time: 884 us; the launch traced here: 874 us
  waiting for transfers between devices  330 us (37%)
  matrix products  210 us (24%)
  starting transfers between devices  117 us (13%)
  local copies, waits for them, and re-layouts  87.4 us (10%)
  other arithmetic  84.4 us (10%)
  blocking collectives  29.1 us (3%)
  between operations  17.1 us (2%)
    ppermute x53, waiting for transfers between devices, at_offset(): return lax.ppermute(arr, 'expert', pairs)  246 us
    ppermute x53, starting transfers between devices, at_offset(): return lax.ppermute(arr, 'expert', pairs)  53.7 us
    unnamed x271, local copies, waits for them, and re-layouts  50.5 us
    all_to_all x2, waiting for transfers between devices, to_owners(): lax.all_to_all(columns.T, 'expert', split_axis=0, concat_axis=0, tiled=True)  44 us
    dot_general x32, matrix products, on_device(): jnp.dot(select[o].astype(brain_float_half), rows[o], preferred_element_ty...  40.1 us
    ppermute x11, waiting for transfers between devices, swap_dp(): return lax.ppermute(arr, 'dp', [(0, 1), (1, 0)])  38.5 us
    all_gather x1, blocking collectives, on_device(): lax.all_gather(jnp.concatenate([attn_gain[None], ffn_gain[None], w_router...  29.1 us
    all_to_all x1, starting transfers between devices, on_device(): lax.all_to_all(returned_gates, 'expert', split_axis=0, concat_axis=0, til...  24.7 us
  transfers between devices with their start and end apart: 71, of which 24 were waited for; matrix products, arithmetic and copies ran while one was open for 29% of the time, Pallas kernels for 0%

profile of v2, /device:TPU:0, one launch (start us, length us, event | category | flops | bytes accessed | tf_op | source)
XLA Modules:
  0.0 874.2 jit_solution(14150039081536675101)
XLA Ops:
  17.9 29.1 %all_gather.6 = bf16[18,1024]{1,0:T(8,128)(2,1)S(1)} all-gather(bf16[18,512]{1,0:T(8,128)(2,1)S(1)} %pad_maximum_fusion.13), channel_id=1, replica_groups=mesh['dp'=2,'expert'=16] {'dp'}, dimensions={1}, use_global_device_ids=true | all-gather | bytes 55296 | tf_op jit(solution)/shard_map/all_gather | solution.py:200
  62.8 8.0 fusion.396
  70.8 8.4 exponential_reduce_fusion
  79.2 8.6 fusion.52
  100.5 42.5 %all-to-all-done.2 = f32[16,1,512]{2,1,0:T(1,128)S(1)} async-done(((f32[16,1,512]{2,1,0:T(1,128)}), f32[16,1,512]{2,1,0:T(1,128)S(1)}, u32[]{:S(2)}, u32[]{:S(2)}) %all-to-all-start.2) | async-done | bytes 32800 | tf_op jit(solution)/shard_map/all_to_all | solution.py:229
  143.1 10.9 %all-to-all-start = ((f32[16,1,512]{2,1,0:T(1,128)}), f32[16,1,512]{2,1,0:T(1,128)S(1)}, u32[]{:S(2)}, u32[]{:S(2)}) async-start(f32[16,1,512]{2,1,0:T(1,128)} %copy.94), calls=%async_computation | async-start | bytes 65536 | tf_op jit(solution)/shard_map/all_to_all | solution.py:229
  167.8 36.7 %collective-permute-done.9 = bf16[512,1024]{1,0:T(8,128)(2,1)} collective-permute-done((bf16[512,1024]{1,0:T(8,128)(2,1)S(1)}, bf16[512,1024]{1,0:T(8,128)(2,1)}, u32[]{:S(2)}, u32[]{:S(2)}) %collective-permute-start.9) | collective-permute-done | bytes 1048608 | tf_op jit(solution)/shard_map/ppermute | solution.py:64
  212.4 20.3 %collective-permute-done.11 = bf16[512,1024]{1,0:T(8,128)(2,1)S(1)} collective-permute-done((bf16[512,1024]{1,0:T(8,128)(2,1)}, bf16[512,1024]{1,0:T(8,128)(2,1)S(1)}, u32[]{:S(2)}, u32[]{:S(2)}) %collective-permute-start.11) | collective-permute-done | bytes 1048608 | tf_op jit(solution)/shard_map/ppermute | solution.py:64
  233.8 21.1 %collective-permute-done.21 = bf16[512,1024]{1,0:T(8,128)(2,1)S(1)} collective-permute-done((bf16[512,1024]{1,0:T(8,128)(2,1)S(1)}, bf16[512,1024]{1,0:T(8,128)(2,1)S(1)}, u32[]{:S(2)}, u32[]{:S(2)}) %collective-permute-start.21) | collective-permute-done | bytes 1048608 | tf_op jit(solution)/shard_map/ppermute | solution.py:64
  261.5 4.6 fusion.387
  271.3 4.6 fusion.386
  295.5 8.1 fusion.5
  317.7 7.8 fusion.8
  328.1 7.6 multiply_convert_fusion.1
  335.8 6.9 convolution_convert_fusion.3
  347.8 7.4 multiply_convert_fusion.3
  355.3 6.9 convolution_convert_fusion.4
  370.1 5.2 fusion.6
  378.0 24.7 %all-to-all-start.1 = ((f32[16,1,512]{2,1,0:T(1,128)}), f32[16,1,512]{2,1,0:T(1,128)S(1)}, u32[]{:S(2)}, u32[]{:S(2)}) async-start(f32[16,1,512]{2,1,0:T(1,128)} %copy.97), calls=%async_computation.1 | async-start | bytes 65536 | tf_op jit(solution)/shard_map/all_to_all | solution.py:362
  438.1 19.4 %collective-permute-done.25 = bf16[512,1024]{1,0:T(8,128)(2,1)S(1)} collective-permute-done((bf16[512,1024]{1,0:T(8,128)(2,1)S(1)}, bf16[512,1024]{1,0:T(8,128)(2,1)S(1)}, u32[]{:S(2)}, u32[]{:S(2)}) %collective-permute-start.25) | collective-permute-done | bytes 1048608 | tf_op jit(solution)/shard_map/ppermute | solution.py:64
  460.9 19.1 %collective-permute-done.29 = bf16[512,1024]{1,0:T(8,128)(2,1)S(1)} collective-permute-done((bf16[512,1024]{1,0:T(8,128)(2,1)S(1)}, bf16[512,1024]{1,0:T(8,128)(2,1)S(1)}, u32[]{:S(2)}, u32[]{:S(2)}) %collective-permute-start.29) | collective-permute-done | bytes 1048608 | tf_op jit(solution)/shard_map/ppermute | solution.py:64
  481.4 4.0 collective-permute-start.30
  485.4 17.1 %collective-permute-done.33 = bf16[512,1024]{1,0:T(8,128)(2,1)S(1)} collective-permute-done((bf16[512,1024]{1,0:T(8,128)(2,1)S(1)}, bf16[512,1024]{1,0:T(8,128)(2,1)S(1)}, u32[]{:S(2)}, u32[]{:S(2)}) %collective-permute-start.33) | collective-permute-done | bytes 1048608 | tf_op jit(solution)/shard_map/ppermute | solution.py:64
  510.9 13.6 %collective-permute-done.37 = bf16[512,1024]{1,0:T(8,128)(2,1)S(1)} collective-permute-done((bf16[512,1024]{1,0:T(8,128)(2,1)}, bf16[512,1024]{1,0:T(8,128)(2,1)S(1)}, u32[]{:S(2)}, u32[]{:S(2)}) %collective-permute-start.37) | collective-permute-done | bytes 1048608 | tf_op jit(solution)/shard_map/ppermute | solution.py:64
  524.5 28.2 %collective-permute-done.34 = bf16[512,1024]{1,0:T(8,128)(2,1)} collective-permute-done((bf16[512,1024]{1,0:T(8,128)(2,1)}, bf16[512,1024]{1,0:T(8,128)(2,1)}, u32[]{:S(2)}, u32[]{:S(2)}) %collective-permute-start.34) | collective-permute-done | bytes 1048608 | tf_op jit(solution)/shard_map/ppermute | solution.py:64
  552.7 4.4 add_add_fusion
  557.7 8.2 gather_fusion.3
  565.9 11.5 %convolution_convert_fusion = bf16[16,512,1024]{2,1,0:T(8,128)(2,1)} fusion(bf16[16,256,1024]{2,1,0:T(8,128)(2,1)} %gather_fusion.3, f32[16,512]{1,0:T(8,128)S(1)} %gather_fusion.2, f32[256]{0:T(256)S(1)} %iota_convert_fusion), kind=kOutput, calls=%fused_computation.21 | convolution fusion | flops 4305453056 | bytes 25199616 | tf_op jit(solution)/shard_map/nct,ncd->ntd/dot_general | solution.py:378
  577.6 8.5 fusion.19
  586.2 4.6 fusion.40
  597.0 4.3 fusion.49
  609.5 14.7 %fusion = (f32[8,2,512]{2,1,0:T(2,128)}, f32[8,512,512,2]{2,1,3,0:T(8,128)}) fusion(f32[8,2,512,512]{2,3,1,0:T(8,128)} %get-tuple-element.262, f32[8,2,512]{2,1,0:T(2,128)} %bitcast.317, bf16[512,8,64,1]{0,2,3,1:T(8,128)(2,1)S(1)} %bitcast.308, bf16[512,8,2,64]{0,3,2,1:T(8,128)(2,1)} %bitcast.297), kind=kOutput, calls=%fused_computation.8 | convolution fusion | flops 549445632 | bytes 35192832 | tf_op jit(solution)/shard_map/while/body/eval_jaxpr/qkgd,skd->kgqs/dot_general | solution.py:401
  627.3 8.5 fusion.2
  642.0 6.2 broadcast_multiply_fusion
  649.4 5.0 fusion.58
  664.3 12.0 %collective-permute-done.63 = bf16[512,512]{1,0:T(8,128)(2,1)S(1)} collective-permute-done((bf16[512,512]{1,0:T(8,128)(2,1)S(1)}, bf16[512,512]{1,0:T(8,128)(2,1)S(1)}, u32[]{:S(2)}, u32[]{:S(2)}) %collective-permute-start.63) | collective-permute-done | bytes 524320 | tf_op jit(solution)/shard_map/ppermute | solution.py:68
  691.3 5.8 collective-permute-done.51
  697.9 20.6 %collective-permute-done.40 = bf16[512,1024]{0,1:T(8,128)(2,1)S(1)} collective-permute-done((bf16[512,1024]{0,1:T(8,128)(2,1)S(1)}, bf16[512,1024]{0,1:T(8,128)(2,1)S(1)}, u32[]{:S(2)}, u32[]{:S(2)}) %collective-permute-start.40) | collective-permute-done | bytes 1048608 | tf_op jit(solution)/shard_map/ppermute | solution.py:68
  721.2 4.3 collective-permute-start.53
  727.3 5.3 all-to-all-start.3
  748.5 3.8 collective-permute-start.58
  752.3 12.9 %collective-permute-done.42 = bf16[64,1024]{0,1:T(8,128)(2,1)S(1)} collective-permute-done((bf16[64,1024]{0,1:T(8,128)(2,1)S(1)}, bf16[64,1024]{0,1:T(8,128)(2,1)S(1)}, u32[]{:S(2)}, u32[]{:S(2)}) %collective-permute-start.42) | collective-permute-done | bytes 131104 | tf_op jit(solution)/shard_map/ppermute | solution.py:64
  765.2 6.0 collective-permute-done.44
  771.2 21.1 %collective-permute-done.43 = bf16[64,1024]{0,1:T(8,128)(2,1)S(1)} collective-permute-done((bf16[64,1024]{0,1:T(8,128)(2,1)S(1)}, bf16[64,1024]{0,1:T(8,128)(2,1)S(1)}, u32[]{:S(2)}, u32[]{:S(2)}) %collective-permute-start.43) | collective-permute-done | bytes 131104 | tf_op jit(solution)/shard_map/ppermute | solution.py:64
  796.4 7.3 collective-permute-done.47
  803.6 8.7 collective-permute-done.46
  821.6 7.0 all-to-all-start.4
  835.7 8.1 collective-permute-done.59
  (572 shorter events, 287.4 us)
Async XLA Ops:
  7.2 274.6 %all-gather.2.cloned.1.call-start = ((), (), s32[]{:S(2)}) async-start(), calls=%async_computation.6 | async-start | bytes 17825792 | tf_op jit(solution)/shard_map/all_gather | solution.py:239
  9.1 41.1 %collective-permute-start.4 = (bf16[256,1024]{1,0:T(8,128)(2,1)S(1)}, bf16[256,1024]{1,0:T(8,128)(2,1)}, u32[]{:S(2)}, u32[]{:S(2)}) collective-permute-start(bf16[256,1024]{1,0:T(8,128)(2,1)S(1)} %constant_dynamic-slice_fusion.13), channel_id=1, source_target_pairs={{0,16},{16,0},{1,17},{17,1},{2,18},{18,2},{3,19},{19,3},{4,20},{20... | collective-permute-start | bytes 1572872 | tf_op jit(solution)/shard_map/ppermute | solution.py:68
  13.2 35.8 %collective-permute-start = (bf16[256,1024]{1,0:T(8,128)(2,1)S(1)}, bf16[256,1024]{1,0:T(8,128)(2,1)S(1)}, u32[]{:S(2)}, u32[]{:S(2)}) collective-permute-start(bf16[256,1024]{1,0:T(8,128)(2,1)S(1)} %constant_dynamic-slice_fusion.15), channel_id=1, source_target_pairs={{0,16},{16,0},{1,17},{17,1},{2,18},{18,2},{3,19},{19,3},{4,20},{20... | collective-permute-start | bytes 1572872 | tf_op jit(solution)/shard_map/ppermute | solution.py:68
  14.4 36.4 %collective-permute-start.2 = (bf16[256,1024]{1,0:T(8,128)(2,1)S(1)}, bf16[256,1024]{1,0:T(8,128)(2,1)}, u32[]{:S(2)}, u32[]{:S(2)}) collective-permute-start(bf16[256,1024]{1,0:T(8,128)(2,1)S(1)} %constant_dynamic-slice_fusion.14), channel_id=1, source_target_pairs={{0,16},{16,0},{1,17},{17,1},{2,18},{18,2},{3,19},{19,3},{4,20},{20... | collective-permute-start | bytes 1572872 | tf_op jit(solution)/shard_map/ppermute | solution.py:68
  90.9 70.5 %collective-permute-start.15 = (bf16[512,1024]{1,0:T(8,128)(2,1)S(1)}, bf16[512,1024]{1,0:T(8,128)(2,1)}, u32[]{:S(2)}, u32[]{:S(2)}) collective-permute-start(bf16[512,1024]{1,0:T(8,128)(2,1)S(1)} %multiply_convert_fusion.6), channel_id=1, source_target_pairs={{12,0},{13,1},{14,2},{15,3},{0,4},{1,5},{2,6},{3,7},{4,8},{5,9},{6... | collective-permute-start | bytes 3145736 | tf_op jit(solution)/shard_map/ppermute | solution.py:64
  92.8 69.3 %collective-permute-start.7 = (bf16[512,1024]{1,0:T(8,128)(2,1)S(1)}, bf16[512,1024]{1,0:T(8,128)(2,1)}, u32[]{:S(2)}, u32[]{:S(2)}) collective-permute-start(bf16[512,1024]{1,0:T(8,128)(2,1)S(1)} %multiply_convert_fusion.6), channel_id=1, source_target_pairs={{2,0},{3,1},{0,2},{1,3},{6,4},{7,5},{4,6},{5,7},{10,8},{11,9},{8,1... | collective-permute-start | bytes 3145736 | tf_op jit(solution)/shard_map/ppermute | solution.py:64
  95.6 47.5 %all-to-all-start.2 = ((f32[16,1,512]{2,1,0:T(1,128)}), f32[16,1,512]{2,1,0:T(1,128)S(1)}, u32[]{:S(2)}, u32[]{:S(2)}) async-start(f32[16,1,512]{2,1,0:T(1,128)} %copy.98), calls=%async_computation.2 | async-start | bytes 65536 | tf_op jit(solution)/shard_map/all_to_all | solution.py:229
  99.4 64.7 %collective-permute-start.6 = (bf16[512,1024]{1,0:T(8,128)(2,1)S(1)}, bf16[512,1024]{1,0:T(8,128)(2,1)}, u32[]{:S(2)}, u32[]{:S(2)}) collective-permute-start(bf16[512,1024]{1,0:T(8,128)(2,1)S(1)} %multiply_convert_fusion.6), channel_id=1, source_target_pairs={{1,0},{0,1},{3,2},{2,3},{5,4},{4,5},{7,6},{6,7},{9,8},{8,9},{11,10... | collective-permute-start | bytes 3145736 | tf_op jit(solution)/shard_map/ppermute | solution.py:64
  154.0 52.5 %collective-permute-start.19 = (bf16[512,1024]{1,0:T(8,128)(2,1)S(1)}, bf16[512,1024]{1,0:T(8,128)(2,1)S(1)}, u32[]{:S(2)}, u32[]{:S(2)}) collective-permute-start(bf16[512,1024]{1,0:T(8,128)(2,1)S(1)} %multiply_convert_fusion.6), channel_id=1, source_target_pairs={{8,0},{9,1},{10,2},{11,3},{12,4},{13,5},{14,6},{15,7},{0,8},{1,9},... | collective-permute-start | bytes 3145736 | tf_op jit(solution)/shard_map/ppermute | solution.py:64
  156.8 47.7 %collective-permute-start.9 = (bf16[512,1024]{1,0:T(8,128)(2,1)S(1)}, bf16[512,1024]{1,0:T(8,128)(2,1)}, u32[]{:S(2)}, u32[]{:S(2)}) collective-permute-start(bf16[512,1024]{1,0:T(8,128)(2,1)S(1)} %multiply_convert_fusion.6), channel_id=1, source_target_pairs={{4,0},{5,1},{6,2},{7,3},{8,4},{9,5},{10,6},{11,7},{12,8},{13,9},{1... | collective-permute-start | bytes 3145736 | tf_op jit(solution)/shard_map/ppermute | solution.py:64
  161.4 44.6 %collective-permute-start.16 = (bf16[512,1024]{1,0:T(8,128)(2,1)}, bf16[512,1024]{1,0:T(8,128)(2,1)S(1)}, u32[]{:S(2)}, u32[]{:S(2)}) collective-permute-start(bf16[512,1024]{1,0:T(8,128)(2,1)} %collective-permute-done.15), channel_id=1, source_target_pairs={{1,0},{0,1},{3,2},{2,3},{5,4},{4,5},{7,6},{6,7},{9,8},{8,9},{11,10... | collective-permute-start | bytes 3145736 | tf_op jit(solution)/shard_map/ppermute | solution.py:64
  162.0 45.5 %collective-permute-start.17 = (bf16[512,1024]{1,0:T(8,128)(2,1)}, bf16[512,1024]{1,0:T(8,128)(2,1)S(1)}, u32[]{:S(2)}, u32[]{:S(2)}) collective-permute-start(bf16[512,1024]{1,0:T(8,128)(2,1)} %collective-permute-done.15), channel_id=1, source_target_pairs={{2,0},{3,1},{0,2},{1,3},{6,4},{7,5},{4,6},{5,7},{10,8},{11,9},{8,1... | collective-permute-start | bytes 3145736 | tf_op jit(solution)/shard_map/ppermute | solution.py:64
  164.1 45.0 %collective-permute-start.8 = (bf16[512,1024]{1,0:T(8,128)(2,1)}, bf16[512,1024]{1,0:T(8,128)(2,1)S(1)}, u32[]{:S(2)}, u32[]{:S(2)}) collective-permute-start(bf16[512,1024]{1,0:T(8,128)(2,1)} %collective-permute-done.7), channel_id=1, source_target_pairs={{1,0},{0,1},{3,2},{2,3},{5,4},{4,5},{7,6},{6,7},{9,8},{8,9},{11,10... | collective-permute-start | bytes 3145736 | tf_op jit(solution)/shard_map/ppermute | solution.py:64
  204.5 91.0 %collective-permute-start.14 = (bf16[512,512]{1,0:T(8,128)(2,1)}, bf16[512,512]{1,0:T(8,128)(2,1)}, u32[]{:S(2)}, u32[]{:S(2)}) collective-permute-start(bf16[512,512]{1,0:T(8,128)(2,1)} %bitcast.44), channel_id=1, source_target_pairs={{0,16},{16,0},{1,17},{17,1},{2,18},{18,2},{3,19},{19,3},{4,20},{20... | collective-permute-start | bytes 1572872 | tf_op jit(solution)/shard_map/ppermute | solution.py:68
  206.5 26.2 %collective-permute-start.11 = (bf16[512,1024]{1,0:T(8,128)(2,1)}, bf16[512,1024]{1,0:T(8,128)(2,1)S(1)}, u32[]{:S(2)}, u32[]{:S(2)}) collective-permute-start(bf16[512,1024]{1,0:T(8,128)(2,1)} %collective-permute-done.9), channel_id=1, source_target_pairs={{2,0},{3,1},{0,2},{1,3},{6,4},{7,5},{4,6},{5,7},{10,8},{11,9},{8,1... | collective-permute-start | bytes 3145736 | tf_op jit(solution)/shard_map/ppermute | solution.py:64
  207.6 47.2 %collective-permute-start.21 = (bf16[512,1024]{1,0:T(8,128)(2,1)S(1)}, bf16[512,1024]{1,0:T(8,128)(2,1)S(1)}, u32[]{:S(2)}, u32[]{:S(2)}) collective-permute-start(bf16[512,1024]{1,0:T(8,128)(2,1)S(1)} %collective-permute-done.19), channel_id=1, source_target_pairs={{2,0},{3,1},{0,2},{1,3},{6,4},{7,5},{4,6},{5,7},{10,8},{11,9},{8,1... | collective-permute-start | bytes 3145736 | tf_op jit(solution)/shard_map/ppermute | solution.py:64
  209.1 45.7 %collective-permute-start.18 = (bf16[512,1024]{1,0:T(8,128)(2,1)S(1)}, bf16[512,1024]{1,0:T(8,128)(2,1)S(1)}, u32[]{:S(2)}, u32[]{:S(2)}) collective-permute-start(bf16[512,1024]{1,0:T(8,128)(2,1)S(1)} %collective-permute-done.17), channel_id=1, source_target_pairs={{1,0},{0,1},{3,2},{2,3},{5,4},{4,5},{7,6},{6,7},{9,8},{8,9},{11,10... | collective-permute-start | bytes 3145736 | tf_op jit(solution)/shard_map/ppermute | solution.py:64
  211.4 44.9 %collective-permute-start.20 = (bf16[512,1024]{1,0:T(8,128)(2,1)S(1)}, bf16[512,1024]{1,0:T(8,128)(2,1)S(1)}, u32[]{:S(2)}, u32[]{:S(2)}) collective-permute-start(bf16[512,1024]{1,0:T(8,128)(2,1)S(1)} %collective-permute-done.19), channel_id=1, source_target_pairs={{1,0},{0,1},{3,2},{2,3},{5,4},{4,5},{7,6},{6,7},{9,8},{8,9},{11,10... | collective-permute-start | bytes 3145736 | tf_op jit(solution)/shard_map/ppermute | solution.py:64
  232.7 28.7 %collective-permute-start.13 = (bf16[512,1024]{1,0:T(8,128)(2,1)S(1)}, bf16[512,1024]{1,0:T(8,128)(2,1)S(1)}, u32[]{:S(2)}, u32[]{:S(2)}) collective-permute-start(bf16[512,1024]{1,0:T(8,128)(2,1)S(1)} %bitcast.439), channel_id=1, source_target_pairs={{0,16},{16,0},{1,17},{17,1},{2,18},{18,2},{3,19},{19,3},{4,20},{20... | collective-permute-start | bytes 3145736 | tf_op jit(solution)/shard_map/ppermute | solution.py:68
  378.0 130.4 %all-to-all-start.1 = ((f32[16,1,512]{2,1,0:T(1,128)}), f32[16,1,512]{2,1,0:T(1,128)S(1)}, u32[]{:S(2)}, u32[]{:S(2)}) async-start(f32[16,1,512]{2,1,0:T(1,128)} %copy.97), calls=%async_computation.1 | async-start | bytes 65536 | tf_op jit(solution)/shard_map/all_to_all | solution.py:362
  402.7 461.6 %reduce-scatter.2.cloned.1.call-start = ((), (), s32[]{:S(2)}) async-start(), calls=%async_computation.7 | async-start | bytes 17825792 | tf_op jit(solution)/shard_map/reduce_scatter | solution.py:381
  403.0 21.7 %collective-permute-start.23 = (bf16[512,1024]{1,0:T(8,128)(2,1)}, bf16[512,1024]{1,0:T(8,128)(2,1)S(1)}, u32[]{:S(2)}, u32[]{:S(2)}) collective-permute-start(bf16[512,1024]{1,0:T(8,128)(2,1)} %convolution_convert_fusion.23), channel_id=1, source_target_pairs={{1,0},{0,1},{3,2},{2,3},{5,4},{4,5},{7,6},{6,7},{9,8},{8,9},{11,10... | collective-permute-start | bytes 3145736 | tf_op jit(solution)/shard_map/ppermute | solution.py:64
  403.5 23.2 %collective-permute-start.24 = (bf16[512,1024]{1,0:T(8,128)(2,1)}, bf16[512,1024]{1,0:T(8,128)(2,1)S(1)}, u32[]{:S(2)}, u32[]{:S(2)}) collective-permute-start(bf16[512,1024]{1,0:T(8,128)(2,1)} %convolution_convert_fusion.21), channel_id=1, source_target_pairs={{1,0},{0,1},{3,2},{2,3},{5,4},{4,5},{7,6},{6,7},{9,8},{8,9},{11,10... | collective-permute-start | bytes 3145736 | tf_op jit(solution)/shard_map/ppermute | solution.py:64
  403.6 105.4 %collective-permute-start.35 = (bf16[512,1024]{1,0:T(8,128)(2,1)}, bf16[512,1024]{1,0:T(8,128)(2,1)}, u32[]{:S(2)}, u32[]{:S(2)}) collective-permute-start(bf16[512,1024]{1,0:T(8,128)(2,1)} %convolution_convert_fusion.11), channel_id=1, source_target_pairs={{1,0},{0,1},{3,2},{2,3},{5,4},{4,5},{7,6},{6,7},{9,8},{8,9},{11,10... | collective-permute-start | bytes 3145736 | tf_op jit(solution)/shard_map/ppermute | solution.py:64
  404.0 24.8 %collective-permute-start.36 = (bf16[512,1024]{1,0:T(8,128)(2,1)}, bf16[512,1024]{1,0:T(8,128)(2,1)S(1)}, u32[]{:S(2)}, u32[]{:S(2)}) collective-permute-start(bf16[512,1024]{1,0:T(8,128)(2,1)} %convolution_convert_fusion.9), channel_id=1, source_target_pairs={{1,0},{0,1},{3,2},{2,3},{5,4},{4,5},{7,6},{6,7},{9,8},{8,9},{11,10... | collective-permute-start | bytes 3145736 | tf_op jit(solution)/shard_map/ppermute | solution.py:64
  404.1 27.5 %collective-permute-start.28 = (bf16[512,1024]{1,0:T(8,128)(2,1)}, bf16[512,1024]{1,0:T(8,128)(2,1)S(1)}, u32[]{:S(2)}, u32[]{:S(2)}) collective-permute-start(bf16[512,1024]{1,0:T(8,128)(2,1)} %convolution_convert_fusion.17), channel_id=1, source_target_pairs={{1,0},{0,1},{3,2},{2,3},{5,4},{4,5},{7,6},{6,7},{9,8},{8,9},{11,10... | collective-permute-start | bytes 3145736 | tf_op jit(solution)/shard_map/ppermute | solution.py:64
  431.6 26.0 %collective-permute-start.25 = (bf16[512,1024]{1,0:T(8,128)(2,1)S(1)}, bf16[512,1024]{1,0:T(8,128)(2,1)S(1)}, u32[]{:S(2)}, u32[]{:S(2)}) collective-permute-start(bf16[512,1024]{1,0:T(8,128)(2,1)S(1)} %add_convert_fusion.14), channel_id=1, source_target_pairs={{2,0},{3,1},{0,2},{1,3},{6,4},{7,5},{4,6},{5,7},{10,8},{11,9},{8,1... | collective-permute-start | bytes 3145736 | tf_op jit(solution)/shard_map/ppermute | solution.py:64
  434.1 46.0 %collective-permute-start.29 = (bf16[512,1024]{1,0:T(8,128)(2,1)S(1)}, bf16[512,1024]{1,0:T(8,128)(2,1)S(1)}, u32[]{:S(2)}, u32[]{:S(2)}) collective-permute-start(bf16[512,1024]{1,0:T(8,128)(2,1)S(1)} %add_convert_fusion.11), channel_id=1, source_target_pairs={{2,0},{3,1},{0,2},{1,3},{6,4},{7,5},{4,6},{5,7},{10,8},{11,9},{8,1... | collective-permute-start | bytes 3145736 | tf_op jit(solution)/shard_map/ppermute | solution.py:64
  434.8 67.7 %collective-permute-start.33 = (bf16[512,1024]{1,0:T(8,128)(2,1)S(1)}, bf16[512,1024]{1,0:T(8,128)(2,1)S(1)}, u32[]{:S(2)}, u32[]{:S(2)}) collective-permute-start(bf16[512,1024]{1,0:T(8,128)(2,1)S(1)} %add_convert_fusion.8), channel_id=1, source_target_pairs={{2,0},{3,1},{0,2},{1,3},{6,4},{7,5},{4,6},{5,7},{10,8},{11,9},{8,1... | collective-permute-start | bytes 3145736 | tf_op jit(solution)/shard_map/ppermute | solution.py:64
  437.4 87.1 %collective-permute-start.37 = (bf16[512,1024]{1,0:T(8,128)(2,1)}, bf16[512,1024]{1,0:T(8,128)(2,1)S(1)}, u32[]{:S(2)}, u32[]{:S(2)}) collective-permute-start(bf16[512,1024]{1,0:T(8,128)(2,1)} %add_convert_fusion.5), channel_id=1, source_target_pairs={{2,0},{3,1},{0,2},{1,3},{6,4},{7,5},{4,6},{5,7},{10,8},{11,9},{8,1... | collective-permute-start | bytes 3145736 | tf_op jit(solution)/shard_map/ppermute | solution.py:64
  458.9 65.6 %collective-permute-start.26 = (bf16[512,1024]{1,0:T(8,128)(2,1)}, bf16[512,1024]{1,0:T(8,128)(2,1)}, u32[]{:S(2)}, u32[]{:S(2)}) collective-permute-start(bf16[512,1024]{1,0:T(8,128)(2,1)} %add_convert_fusion.13), channel_id=1, source_target_pairs={{12,0},{13,1},{14,2},{15,3},{0,4},{1,5},{2,6},{3,7},{4,8},{5,9},{6... | collective-permute-start | bytes 3145736 | tf_op jit(solution)/shard_map/ppermute | solution.py:64
  481.4 43.1 %collective-permute-start.30 = (bf16[512,1024]{1,0:T(8,128)(2,1)}, bf16[512,1024]{1,0:T(8,128)(2,1)}, u32[]{:S(2)}, u32[]{:S(2)}) collective-permute-start(bf16[512,1024]{1,0:T(8,128)(2,1)} %add_convert_fusion.10), channel_id=1, source_target_pairs={{4,0},{5,1},{6,2},{7,3},{8,4},{9,5},{10,6},{11,7},{12,8},{13,9},{1... | collective-permute-start | bytes 3145736 | tf_op jit(solution)/shard_map/ppermute | solution.py:64
  503.9 48.8 %collective-permute-start.34 = (bf16[512,1024]{1,0:T(8,128)(2,1)}, bf16[512,1024]{1,0:T(8,128)(2,1)}, u32[]{:S(2)}, u32[]{:S(2)}) collective-permute-start(bf16[512,1024]{1,0:T(8,128)(2,1)} %add_convert_fusion.7), channel_id=1, source_target_pairs={{8,0},{9,1},{10,2},{11,3},{12,4},{13,5},{14,6},{15,7},{0,8},{1,9},... | collective-permute-start | bytes 3145736 | tf_op jit(solution)/shard_map/ppermute | solution.py:64
  592.0 85.5 %collective-permute-start.62 = (bf16[512,1024]{1,0:T(8,128)(2,1)}, bf16[512,1024]{1,0:T(8,128)(2,1)}, u32[]{:S(2)}, u32[]{:S(2)}) collective-permute-start(bf16[512,1024]{1,0:T(8,128)(2,1)} %dynamic-slice_convert_fusion), channel_id=1, source_target_pairs={{0,16},{16,0},{1,17},{17,1},{2,18},{18,2},{3,19},{19,3},{4,20},{20... | collective-permute-start | bytes 3145736 | tf_op jit(solution)/shard_map/ppermute | solution.py:68
  661.8 20.8 %collective-permute-start.39 = (bf16[1024,1024]{0,1:T(8,128)(2,1)S(1)}, bf16[1024,1024]{0,1:T(8,128)(2,1)S(1)}, u32[]{:S(2)}, u32[]{:S(2)}) collective-permute-start(bf16[1024,1024]{0,1:T(8,128)(2,1)S(1)} %fusion.33), channel_id=1, source_target_pairs={{1,0},{0,1},{3,2},{2,3},{5,4},{4,5},{7,6},{6,7},{9,8},{8,9},{11,10... | collective-permute-start | bytes 6291464 | tf_op jit(solution)/shard_map/ppermute | solution.py:64
  686.0 32.5 %collective-permute-start.40 = (bf16[512,1024]{0,1:T(8,128)(2,1)S(1)}, bf16[512,1024]{0,1:T(8,128)(2,1)S(1)}, u32[]{:S(2)}, u32[]{:S(2)}) collective-permute-start(bf16[512,1024]{0,1:T(8,128)(2,1)S(1)} %constant_dynamic-slice_fusion.12), channel_id=1, source_target_pairs={{0,16},{16,0},{1,17},{17,1},{2,18},{18,2},{3,19},{19,3},{4,20},{20... | collective-permute-start | bytes 3145736 | tf_op jit(solution)/shard_map/ppermute | solution.py:68
  691.1 35.1 %collective-permute-start.38 = (f32[1,512]{1,0:T(1,128)S(1)}, f32[1,512]{1,0:T(1,128)S(1)}, u32[]{:S(2)}, u32[]{:S(2)}) collective-permute-start(f32[1,512]{1,0:T(1,128)S(1)} %bitcast.438), channel_id=1, source_target_pairs={{0,16},{16,0},{1,17},{17,1},{2,18},{18,2},{3,19},{19,3},{4,20},{20... | collective-permute-start | bytes 6152 | tf_op jit(solution)/shard_map/ppermute | solution.py:68
  697.3 23.1 %collective-permute-start.52 = (bf16[256,512]{1,0:T(8,128)(2,1)S(1)}, bf16[256,512]{1,0:T(8,128)(2,1)S(1)}, u32[]{:S(2)}, u32[]{:S(2)}) collective-permute-start(bf16[256,512]{1,0:T(8,128)(2,1)S(1)} %constant_dynamic-slice_fusion.4), channel_id=1, source_target_pairs={{2,0},{3,1},{0,2},{1,3},{6,4},{7,5},{4,6},{5,7},{10,8},{11,9},{8,1... | collective-permute-start | bytes 786440 | tf_op jit(solution)/shard_map/ppermute | solution.py:64
  719.9 22.2 %collective-permute-start.41 = (bf16[256,1024]{0,1:T(8,128)(2,1)S(1)}, bf16[256,1024]{0,1:T(8,128)(2,1)S(1)}, u32[]{:S(2)}, u32[]{:S(2)}) collective-permute-start(bf16[256,1024]{0,1:T(8,128)(2,1)S(1)} %constant_dynamic-slice_fusion.11), channel_id=1, source_target_pairs={{2,0},{3,1},{0,2},{1,3},{6,4},{7,5},{4,6},{5,7},{10,8},{11,9},{8,1... | collective-permute-start | bytes 1572872 | tf_op jit(solution)/shard_map/ppermute | solution.py:64
  726.2 21.4 %collective-permute-start.61 = (f32[17,512]{1,0:T(8,128)S(1)}, f32[17,512]{1,0:T(8,128)}, u32[]{:S(2)}, u32[]{:S(2)}) collective-permute-start(f32[17,512]{1,0:T(8,128)S(1)} %fusion.332), channel_id=1, source_target_pairs={{0,16},{16,0},{1,17},{17,1},{2,18},{18,2},{3,19},{19,3},{4,20},{20... | collective-permute-start | bytes 104456 | tf_op jit(solution)/shard_map/ppermute | solution.py:68
  727.3 93.3 %all-to-all-start.3 = ((f32[16,1,512]{2,1,0:T(1,128)}), f32[16,1,512]{2,1,0:T(1,128)}, u32[]{:S(2)}, u32[]{:S(2)}) async-start(f32[16,1,512]{2,1,0:T(1,128)} %broadcast_in_dim.469), calls=%async_computation.4 | async-start | bytes 65536 | tf_op jit(solution)/shard_map/all_to_all | solution.py:470
  743.6 21.5 %collective-permute-start.42 = (bf16[64,1024]{0,1:T(8,128)(2,1)S(1)}, bf16[64,1024]{0,1:T(8,128)(2,1)S(1)}, u32[]{:S(2)}, u32[]{:S(2)}) collective-permute-start(bf16[64,1024]{0,1:T(8,128)(2,1)S(1)} %get-tuple-element.197), channel_id=1, source_target_pairs={{4,0},{5,1},{6,2},{7,3},{8,4},{9,5},{10,6},{11,7},{12,8},{13,9},{1... | collective-permute-start | bytes 393224 | tf_op jit(solution)/shard_map/ppermute | solution.py:64
  746.9 24.2 %collective-permute-start.44 = (bf16[64,1024]{0,1:T(8,128)(2,1)S(1)}, bf16[64,1024]{0,1:T(8,128)(2,1)S(1)}, u32[]{:S(2)}, u32[]{:S(2)}) collective-permute-start(bf16[64,1024]{0,1:T(8,128)(2,1)S(1)} %get-tuple-element.198), channel_id=1, source_target_pairs={{12,0},{13,1},{14,2},{15,3},{0,4},{1,5},{2,6},{3,7},{4,8},{5,9},{6... | collective-permute-start | bytes 393224 | tf_op jit(solution)/shard_map/ppermute | solution.py:64
  746.9 45.3 %collective-permute-start.43 = (bf16[64,1024]{0,1:T(8,128)(2,1)S(1)}, bf16[64,1024]{0,1:T(8,128)(2,1)S(1)}, u32[]{:S(2)}, u32[]{:S(2)}) collective-permute-start(bf16[64,1024]{0,1:T(8,128)(2,1)S(1)} %get-tuple-element.199), channel_id=1, source_target_pairs={{8,0},{9,1},{10,2},{11,3},{12,4},{13,5},{14,6},{15,7},{0,8},{1,9},... | collective-permute-start | bytes 393224 | tf_op jit(solution)/shard_map/ppermute | solution.py:64
  748.5 47.9 %collective-permute-start.58 = (bf16[64,512]{1,0:T(8,128)(2,1)S(1)}, bf16[64,512]{1,0:T(8,128)(2,1)S(1)}, u32[]{:S(2)}, u32[]{:S(2)}) collective-permute-start(bf16[64,512]{1,0:T(8,128)(2,1)S(1)} %get-tuple-element.182), channel_id=1, source_target_pairs={{12,0},{13,1},{14,2},{15,3},{0,4},{1,5},{2,6},{3,7},{4,8},{5,9},{6... | collective-permute-start | bytes 196616 | tf_op jit(solution)/shard_map/ppermute | solution.py:64
  752.3 44.0 %collective-permute-start.57 = (bf16[64,512]{1,0:T(8,128)(2,1)S(1)}, bf16[64,512]{1,0:T(8,128)(2,1)S(1)}, u32[]{:S(2)}, u32[]{:S(2)}) collective-permute-start(bf16[64,512]{1,0:T(8,128)(2,1)S(1)} %get-tuple-element.182), channel_id=1, source_target_pairs={{8,0},{9,1},{10,2},{11,3},{12,4},{13,5},{14,6},{15,7},{0,8},{1,9},... | collective-permute-start | bytes 196616 | tf_op jit(solution)/shard_map/ppermute | solution.py:64
  792.5 19.8 %collective-permute-start.46 = (bf16[64,1024]{0,1:T(8,128)(2,1)S(1)}, bf16[64,1024]{0,1:T(8,128)(2,1)S(1)}, u32[]{:S(2)}, u32[]{:S(2)}) collective-permute-start(bf16[64,1024]{0,1:T(8,128)(2,1)S(1)} %add_convert_fusion.19), channel_id=1, source_target_pairs={{8,0},{9,1},{10,2},{11,3},{12,4},{13,5},{14,6},{15,7},{0,8},{1,9},... | collective-permute-start | bytes 393224 | tf_op jit(solution)/shard_map/ppermute | solution.py:64
  821.6 27.5 %all-to-all-start.4 = ((f32[16,17,512]{2,1,0:T(8,128)}), f32[16,17,512]{2,1,0:T(8,128)S(1)}, u32[]{:S(2)}, u32[]{:S(2)}) async-start(f32[16,17,512]{2,1,0:T(8,128)} %broadcast_in_dim.471), calls=%async_computation.5 | async-start | bytes 1572864 | tf_op jit(solution)/shard_map/all_to_all | solution.py:470
  (139 other events, 2169.3 us)
Sparse Core Ops, SparseCore 0:
  10.2 151.0 all-gather.1
  577.6 216.2 reduce-scatter.1
